TPU v7x, 128 devices: a whole 4x4x4 slice. The times are simulated.
128 devices in a mesh: vid: 16 (over y_hi, z, core), tm: 8 (over y_lo, x).
Axes of the slice: x: 4, y: 4 (y_hi: 2, y_lo: 2; y = y_hi * 2 + y_lo), z: 4, core: 2. Of those that a mesh axis runs over, the one named last changes fastest.
Arguments:
- tokens: bfloat16 [16, 1024, 16, 1024], P('vid', 'tm'), may hold values from -6 to 6
- norm_gain: float32 [1024], replicated, may hold values from 0.1 to 1.9
- w_qkv: bfloat16 [1024, 3072], replicated, may hold values from -0.1875 to 0.1875
- w_out: bfloat16 [1024, 1024], replicated, may hold values from -0.1875 to 0.1875
- w_proj: bfloat16 [1024, 2048], replicated, may hold values from -0.1875 to 0.1875
- offsets: int32 [16, 1024], P('vid', 'tm'), may hold values from -8 to 8, as said below
- negatives: int32 [16, 1024, 8], P(None, 'tm'), may hold values from 0 to 15, as said below
- valid: int32 [16], replicated, may hold values from 528 to 1024
Outputs:
- embeddings: bfloat16 [16, 1024, 2048], P('vid', 'tm')
- losses: float32 [16, 1024], P('vid', 'tm')
Inputs may be any that keep to these rules, and one draw needn't show every extreme that they name: `negatives`: a negative id never equals the anchor's own video. `offsets`: an offset is never 0.
All inputs are finite; a program needn't handle non-finite values.
Results may differ from a plain program's by a relative error of at most 0.015.
Values may be sent and summed in bfloat16 or wider, within the bound.
A program may use at most 128 MiB of HBM per device.

v0:
```python
import jax
import jax.numpy as jnp
from jax import lax
from jax.sharding import PartitionSpec as P

HEADS = 16
WINDOW = 16
REACH = 8


def extended_2(value, sides, width):
    for axis, dim in sides:
        count, length = (lax.axis_size(axis), value.shape[dim])
        up = [(i, (i + 1) % count) for i in range(count - 1)]
        down = [(j, i) for i, j in up]
        last = lax.slice_in_dim(value, length - width, length, axis=dim)
        first = lax.slice_in_dim(value, 0, width, axis=dim)
        before = lax.ppermute(last, axis, up)
        after = lax.ppermute(first, axis, down)
        value = jnp.concatenate([before, value, after], axis=dim)
    return value


def attend(query, keys, values, first, total, lengths, window):
    count = query.shape[1]
    span = keys.shape[1]
    heads = HEADS
    size = query.shape[-1] // heads
    shape_q = query.shape[:3] + (heads, size)
    shape_k = keys.shape[:3] + (heads, size)
    query4 = query.reshape(shape_q)
    keys4 = keys.reshape(shape_k)
    values4 = values.reshape(shape_k)
    scores = jnp.einsum("vfphc,vgphc->vphfg", query4, keys4, preferred_element_type=jnp.float32)
    scores = scores / jnp.sqrt(jnp.float32(size))
    rows = first + jnp.arange(count)[:, None]
    cols = first - window + jnp.arange(span)[None, :]
    inside = (jnp.abs(rows - cols) <= window) & (cols >= 0) & (cols < total)
    allowed = inside[None] & ((cols[None] < lengths[:, None, None]) | (cols == rows)[None])
    scores = jnp.where(allowed[:, None, None], scores, -1e30)
    probs = jax.nn.softmax(scores, axis=-1).astype(jnp.bfloat16)
    attended_tokens = jnp.einsum(
        "vphfg,vgphc->vfphc", probs, values4, preferred_element_type=jnp.float32
    )
    return attended_tokens.astype(jnp.bfloat16).reshape(query.shape)


def local(tokens, norm_gain, w_qkv, w_out, w_proj, offsets, negatives, valid):
    videos_here = tokens.shape[0]
    count = tokens.shape[1]
    width = tokens.shape[3]
    total = lax.axis_size("tm") * count
    first = lax.axis_index("tm") * count
    base = lax.axis_index("vid") * videos_here
    lengths = lax.dynamic_slice_in_dim(valid, base, videos_here, 0)
    xf = tokens.astype(jnp.float32)
    scale = lax.rsqrt(jnp.mean(xf * xf, axis=-1, keepdims=True) + 1e-05)
    normed = (xf * scale * norm_gain).astype(jnp.bfloat16)
    qkv = jnp.einsum("vfpd,de->vfpe", normed, w_qkv, preferred_element_type=jnp.float32).astype(
        jnp.bfloat16
    )
    query = qkv[..., :width]
    paired = extended_2(qkv[..., width:], (("tm", 1),), WINDOW)
    attended_tokens = attend(
        query, paired[..., :width], paired[..., width:], first, total, lengths, WINDOW
    )
    output = jnp.einsum("vfpd,de->vfpe", attended_tokens, w_out, preferred_element_type=jnp.float32)
    pooled = jnp.mean(xf + output, axis=2).astype(jnp.bfloat16)
    embeddings = jnp.einsum(
        "vfd,de->vfe", pooled, w_proj, preferred_element_type=jnp.float32
    ).astype(jnp.bfloat16)
    factor = 8.0 / jnp.sqrt(jnp.float32(embeddings.shape[-1]))
    frame_ids = first + jnp.arange(count)
    ahead = frame_ids[None, :] + offsets
    inside_video = (ahead >= 0) & (ahead < lengths[:, None])
    positive = jnp.where(inside_video, ahead, frame_ids[None, :] - offsets)
    extended = extended_2(embeddings, (("tm", 1),), REACH)
    location_index = positive - first + REACH
    near_scores = jnp.einsum(
        "vfe,vse->vfs", embeddings, extended, preferred_element_type=jnp.float32
    )
    slots = jnp.arange(extended.shape[1])
    pick_mask = (location_index[:, :, None] == slots[None, None, :]).astype(jnp.float32)
    pos = jnp.sum(near_scores * pick_mask, axis=-1) * factor
    own_video_index = lax.dynamic_slice_in_dim(negatives, base, videos_here, 0)
    token_piece = lax.all_gather(embeddings, "vid", axis=0, tiled=True)
    similarity_scores = jnp.einsum(
        "tim,yim->tiy", embeddings, token_piece, preferred_element_type=jnp.float32
    )
    owners = jnp.arange(token_piece.shape[0])
    selection_mask = (own_video_index[..., None] == owners).astype(jnp.float32)
    negative_sample = jnp.einsum("imtg,img->imt", selection_mask, similarity_scores)
    negative_sample = negative_sample * factor
    table = jnp.arange(valid.shape[0])
    neg_lengths = jnp.sum(jnp.where(own_video_index[..., None] == table, valid, 0), axis=-1)
    negative_sample = jnp.where(frame_ids[None, :, None] < neg_lengths, negative_sample, -1e30)
    every = jnp.concatenate([pos[:, :, None], negative_sample], axis=-1)
    top = jnp.max(every, axis=-1)
    lse = top + jnp.log(jnp.sum(jnp.exp(every - top[:, :, None]), axis=-1))
    losses = jnp.where(frame_ids[None, :] < lengths[:, None], lse - pos, 0.0)
    return (embeddings, losses)


def solution(mesh):
    placed = (
        P("vid", "tm", None, None),
        P(),
        P(),
        P(),
        P(),
        P("vid", "tm"),
        P(None, "tm", None),
        P(),
    )
    return jax.shard_map(
        local,
        mesh=mesh,
        in_specs=placed,
        out_specs=(P("vid", "tm", None), P("vid", "tm")),
        check_vma=False,
    )
```

profile of v0, /device:TPU:1, one launch (start us, length us, event | category | flops | bytes accessed | tf_op | source)
XLA Modules:
  0.0 252.6 jit_solution(7556669569164971848)
XLA Ops:
  7.2 4.7 %fusion.6 = f32[128,16]{0,1:T(8,128)S(1)} fusion(bf16[1,128,16,1024]{3,2,1,0:T(8,128)(2,1)} %param.8), kind=kLoop, calls=%fused_computation.14 | loop fusion | flops 6289408 | bytes 4202496 | tf_op jit(solution)/shard_map/reduce_sum | solution.py:57
  11.9 27.8 %convert_bitcast_fusion = bf16[1,128,16,3072]{3,1,2,0:T(8,128)(2,1)} fusion(bf16[1024,3072]{1,0:T(8,128)(2,1)} %param.10, f32[1024]{0:T(1024)} %param.9, f32[128,16]{0,1:T(8,128)S(1)} %add_rsqrt_fusion, bf16[1,128,16,1024]{3,2,1,0:T(8,128)(2,1)} %param.8), kind=kOutput, calls=%fused_computation.5 | convolution fusion | flops 12899581952 | bytes 23080960 | tf_op jit(solution)/shard_map/vfpd,de->vfpe/dot_general | solution.py:59
  39.7 3.1 %fusion.55 = (bf16[1,16,16,2048]{3,1,2,0:T(8,128)(2,1)}, bf16[1,16,16,2048]{3,1,2,0:T(8,128)(2,1)}) fusion(bf16[1,128,16,3072]{3,1,2,0:T(8,128)(2,1)} %convert_bitcast_fusion), kind=kLoop, calls=%fused_computation.77 | loop fusion | bytes 4194304 | tf_op jit(solution)/shard_map/slice | solution.py:16
  42.8 4.0 %collective-permute-start = (bf16[1,16,16,2048]{3,1,2,0:T(8,128)(2,1)}, bf16[1,16,16,2048]{3,1,2,0:T(8,128)(2,1)S(1)}, u32[]{:S(2)}, u32[]{:S(2)}) collective-permute-start(bf16[1,16,16,2048]{3,1,2,0:T(8,128)(2,1)} %get-tuple-element.4), channel_id=1, source_target_pairs={{0,1},{1,2},{2,3},{3,4},{4,5},{5,6},{6,7},{8,9},{9,10},{10,11},{11... | collective-permute-start | bytes 3145736 | tf_op jit(solution)/shard_map/ppermute | solution.py:18
  46.8 1.3 collective-permute-start.1
  48.1 8.2 %slice.35 = bf16[1,128,16,2048]{3,1,2,0:T(8,128)(2,1)} slice(bf16[1,128,16,3072]{3,1,2,0:T(8,128)(2,1)} %convert_bitcast_fusion), slice={[0:1], [0:128], [0:16], [1024:3072]} | slice | bytes 16777216 | tf_op jit(solution)/shard_map/slice | solution.py:63
  56.3 4.8 %slice.38 = bf16[1,128,16,1024]{3,1,2,0:T(8,128)(2,1)} slice(bf16[1,128,16,3072]{3,1,2,0:T(8,128)(2,1)} %convert_bitcast_fusion), slice={[0:1], [0:128], [0:16], [0:1024]} | slice | bytes 8388608 | tf_op jit(solution)/shard_map/slice | solution.py:62
  61.1 6.4 %copy.38 = bf16[1,128,16,1024]{1,3,2,0:T(8,128)(2,1)} copy(bf16[1,128,16,1024]{3,1,2,0:T(8,128)(2,1)} %slice.38) | data formatting | bytes 8388608 | tf_op jit(solution)/shard_map/slice | solution.py:62
  67.5 0.6 dynamic_slice.6
  68.1 0.6 fusion.43
  68.6 0.2 fusion.39
  68.8 3.9 %collective-permute-done.1 = bf16[1,16,16,2048]{3,1,2,0:T(8,128)(2,1)} collective-permute-done((bf16[1,16,16,2048]{3,1,2,0:T(8,128)(2,1)}, bf16[1,16,16,2048]{3,1,2,0:T(8,128)(2,1)}, u32[]{:S(2)}, u32[]{:S(2)}) %collective-permute-start.1) | collective-permute-done | bytes 1048608 | tf_op jit(solution)/shard_map/ppermute | solution.py:19
  72.7 11.5 %pad_maximum_fusion = bf16[1,160,16,2048]{3,1,2,0:T(8,128)(2,1)} fusion(bf16[1,16,16,2048]{3,1,2,0:T(8,128)(2,1)} %collective-permute-done.1, bf16[1,128,16,2048]{3,1,2,0:T(8,128)(2,1)} %slice.35, bf16[1,16,16,2048]{3,1,2,0:T(8,128)(2,1)S(1)} %collective-permute-done), kind=kLoop, calls=%fused_computation.9 | loop fusion | flops 31457280 | bytes 20971520 | tf_op jit(solution)/shard_map/concatenate | solution.py:20
  84.2 10.0 %fusion.56 = (bf16[1,160,16,1024]{3,1,2,0:T(8,128)(2,1)}, bf16[1,160,16,1024]{3,1,2,0:T(8,128)(2,1)}) fusion(bf16[1,160,16,2048]{3,1,2,0:T(8,128)(2,1)} %pad_maximum_fusion), kind=kLoop, calls=%fused_computation.78 | loop fusion | bytes 20971520 | tf_op jit(solution)/shard_map/slice | solution.py:65
  94.2 10.7 %copy.57 = bf16[1,160,16,1024]{1,3,2,0:T(8,128)(2,1)} copy(bf16[1,160,16,1024]{3,1,2,0:T(8,128)(2,1)} %get-tuple-element.6) | data formatting | bytes 10485760 | tf_op jit(solution)/shard_map/reshape.14
  104.9 10.7 %copy.56 = bf16[1,160,16,1024]{1,3,2,0:T(8,128)(2,1)} copy(bf16[1,160,16,1024]{3,1,2,0:T(8,128)(2,1)} %get-tuple-element.7) | data formatting | bytes 10485760 | tf_op jit(solution)/shard_map/reshape.18
  115.6 14.7 %fusion.58 = (f32[16,16,128]{2,1,0:T(8,128)S(1)}, f32[16,16,128,160]{2,3,1,0:T(8,128)}) fusion(pred[128,160]{0,1:T(8,128)(4,1)S(1)} %fusion.39, bf16[128,16,16,64]{0,3,2,1:T(8,128)(2,1)} %bitcast.74, bf16[160,16,16,64]{0,3,2,1:T(8,128)(2,1)} %bitcast.72), kind=kOutput, calls=%fused_computation.80 | convolution fusion | flops 692060288 | bytes 30560256 | tf_op jit(solution)/shard_map/sub | solution.py:41
  130.3 13.2 %fusion.18 = bf16[16,16,64,128]{3,2,1,0:T(8,128)(2,1)} fusion(bf16[160,16,16,64]{0,3,2,1:T(8,128)(2,1)} %bitcast.73, f32[16,16,128,160]{2,3,1,0:T(8,128)} %get-tuple-element.13, f32[16,16,128]{2,1,0:T(8,128)S(1)} %get-tuple-element.12), kind=kOutput, calls=%fused_computation.25 | convolution fusion | flops 683671552 | bytes 30539776 | tf_op jit(solution)/shard_map/vphfg,vgphc->vfphc/dot_general | solution.py:42
  143.6 12.3 %fusion.9 = f32[128,1024]{1,0:T(8,128)S(1)} fusion(bf16[128,16,1024]{0,2,1:T(8,128)(2,1)} %bitcast.81, bf16[1,128,16,1024]{3,2,1,0:T(8,128)(2,1)S(1)} %copy-done.2, bf16[1024,1024]{1,0:T(8,128)(2,1)S(1)} %copy-done), kind=kOutput, calls=%fused_computation.17 | convolution fusion | flops 4301127680 | bytes 11010048 | tf_op jit(solution)/shard_map/vfpd,de->vfpe/dot_general | solution.py:67
  155.9 1.5 convolution_convert_fusion
  157.4 0.7 dynamic-slice_bitcast_fusion
  158.1 0.6 add_bitcast_fusion
  158.7 0.8 fusion.57
  159.5 3.0 %collective-permute-start.2 = (bf16[1,8,2048]{2,1,0:T(8,128)(2,1)S(1)}, bf16[1,8,2048]{2,1,0:T(8,128)(2,1)S(1)}, u32[]{:S(2)}, u32[]{:S(2)}) collective-permute-start(bf16[1,8,2048]{2,1,0:T(8,128)(2,1)S(1)} %get-tuple-element.8), channel_id=1, source_target_pairs={{0,1},{1,2},{2,3},{3,4},{4,5},{5,6},{6,7},{8,9},{9,10},{10,11},{11... | collective-permute-start | bytes 98312 | tf_op jit(solution)/shard_map/ppermute | solution.py:18
  162.5 1.3 collective-permute-start.3
  163.8 0.1 select_reduce_fusion
  163.9 0.1 copy.43
  164.0 3.2 %collective-permute-done.3 = bf16[1,8,2048]{2,1,0:T(8,128)(2,1)S(1)} collective-permute-done((bf16[1,8,2048]{2,1,0:T(8,128)(2,1)S(1)}, bf16[1,8,2048]{2,1,0:T(8,128)(2,1)S(1)}, u32[]{:S(2)}, u32[]{:S(2)}) %collective-permute-start.3) | collective-permute-done | bytes 32800 | tf_op jit(solution)/shard_map/ppermute | solution.py:19
  167.2 1.6 fusion.25
  168.7 67.5 %all-gather.3.cloned.1.call-done = bf16[2048,2048]{1,0:T(8,128)(2,1)} async-done(((bf16[128,2048]{1,0:T(8,128)(2,1)}), bf16[2048,2048]{1,0:T(8,128)(2,1)}) %all-gather.3.cloned.1.call-update) | async-done | bytes 8388624 | tf_op jit(solution)/shard_map/all_gather | solution.py:86
  236.2 8.3 %fusion.27 = f32[128,1,8]{2,1,0:T(1,128)S(1)} fusion(bf16[16,128,2048]{2,1,0:T(8,128)(2,1)} %bitcast.80, bf16[128,2048,1]{1,0,2:T(8,128)(2,1)} %bitcast.77, s32[128,8]{1,0:T(8,128)S(1)} %copy.43), kind=kOutput, calls=%fused_computation.32 | convolution fusion | flops 8437760 | bytes 8921088 | tf_op jit(solution)/shard_map/imtg,img->imt/dot_general | solution.py:92
  244.7 1.1 compare_select_fusion
  (22 shorter events, 0.3 us)
Async XLA Ops:
  7.2 136.4 %copy-start = (bf16[1024,1024]{1,0:T(8,128)(2,1)S(1)}, bf16[1024,1024]{1,0:T(8,128)(2,1)}, u32[]{:S(2)}) copy-start(bf16[1024,1024]{1,0:T(8,128)(2,1)} %param.11) | copy-start | bytes 6291460
  7.2 229.0 %all-gather.3.cloned.1.call-start = ((), (), s32[]{:S(2)}) async-start(), calls=%async_computation | async-start | bytes 8912896 | tf_op jit(solution)/shard_map/all_gather | solution.py:86
  42.8 26.1 %collective-permute-start = (bf16[1,16,16,2048]{3,1,2,0:T(8,128)(2,1)}, bf16[1,16,16,2048]{3,1,2,0:T(8,128)(2,1)S(1)}, u32[]{:S(2)}, u32[]{:S(2)}) collective-permute-start(bf16[1,16,16,2048]{3,1,2,0:T(8,128)(2,1)} %get-tuple-element.4), channel_id=1, source_target_pairs={{0,1},{1,2},{2,3},{3,4},{4,5},{5,6},{6,7},{8,9},{9,10},{10,11},{11... | collective-permute-start | bytes 3145736 | tf_op jit(solution)/shard_map/ppermute | solution.py:18
  46.8 25.9 %collective-permute-start.1 = (bf16[1,16,16,2048]{3,1,2,0:T(8,128)(2,1)}, bf16[1,16,16,2048]{3,1,2,0:T(8,128)(2,1)}, u32[]{:S(2)}, u32[]{:S(2)}) collective-permute-start(bf16[1,16,16,2048]{3,1,2,0:T(8,128)(2,1)} %get-tuple-element.5), channel_id=1, source_target_pairs={{1,0},{2,1},{3,2},{4,3},{5,4},{6,5},{7,6},{9,8},{10,9},{11,10},{12... | collective-permute-start | bytes 3145736 | tf_op jit(solution)/shard_map/ppermute | solution.py:19
  56.3 11.2 %copy-start.3 = (s32[16]{0:T(128)S(1)}, s32[16]{0:T(128)}, u32[]{:S(2)}) copy-start(s32[16]{0:T(128)} %param.15) | copy-start | bytes 196
  130.3 13.2 %copy-start.2 = (bf16[1,128,16,1024]{3,2,1,0:T(8,128)(2,1)S(1)}, bf16[1,128,16,1024]{3,2,1,0:T(8,128)(2,1)}, u32[]{:S(2)}) copy-start(bf16[1,128,16,1024]{3,2,1,0:T(8,128)(2,1)} %param.8) | copy-start | bytes 12582916
  143.5 12.3 %copy-start.1 = (bf16[1024,2048]{1,0:T(8,128)(2,1)S(1)}, bf16[1024,2048]{1,0:T(8,128)(2,1)}, u32[]{:S(2)}) copy-start(bf16[1024,2048]{1,0:T(8,128)(2,1)} %param.12) | copy-start | bytes 12582916
  143.6 14.6 %copy-start.4 = (s32[1,128]{1,0:T(1,128)S(1)}, s32[1,128]{1,0:T(1,128)}, u32[]{:S(2)}) copy-start(s32[1,128]{1,0:T(1,128)} %param.13) | copy-start | bytes 1540
  159.5 4.5 %collective-permute-start.2 = (bf16[1,8,2048]{2,1,0:T(8,128)(2,1)S(1)}, bf16[1,8,2048]{2,1,0:T(8,128)(2,1)S(1)}, u32[]{:S(2)}, u32[]{:S(2)}) collective-permute-start(bf16[1,8,2048]{2,1,0:T(8,128)(2,1)S(1)} %get-tuple-element.8), channel_id=1, source_target_pairs={{0,1},{1,2},{2,3},{3,4},{4,5},{5,6},{6,7},{8,9},{9,10},{10,11},{11... | collective-permute-start | bytes 98312 | tf_op jit(solution)/shard_map/ppermute | solution.py:18
  162.5 4.7 %collective-permute-start.3 = (bf16[1,8,2048]{2,1,0:T(8,128)(2,1)S(1)}, bf16[1,8,2048]{2,1,0:T(8,128)(2,1)S(1)}, u32[]{:S(2)}, u32[]{:S(2)}) collective-permute-start(bf16[1,8,2048]{2,1,0:T(8,128)(2,1)S(1)} %get-tuple-element.9), channel_id=1, source_target_pairs={{1,0},{2,1},{3,2},{4,3},{5,4},{6,5},{7,6},{9,8},{10,9},{11,10},{12... | collective-permute-start | bytes 98312 | tf_op jit(solution)/shard_map/ppermute | solution.py:19
Sparse Core Ops, SparseCore 0:
  157.6 78.6 all-gather.2
where the time goes:
time: 254 us; the launch traced here: 253 us
  matrix products  79.4 us (31%)
  waiting for transfers between devices  74.6 us (29%)
  local copies, waits for them, and re-layouts  56.1 us (22%)
  other arithmetic  18.7 us (7%)
  between operations  14.2 us (6%)
  starting transfers between devices  9.66 us (4%)
    all_gather x1, waiting for transfers between devices, local(): token_piece = lax.all_gather(embeddings, 'vid', axis=0, tiled=True)  67.5 us
    dot_general x1, matrix products, local(): jnp.einsum('vfpd,de->vfpe', normed, w_qkv, preferred_element_type=jnp.flo...  27.8 us
    another operation x2, local copies, waits for them, and re-layouts  21.4 us
    sub x1, matrix products, attend(): probs = jax.nn.softmax(scores, axis=-1).astype(jnp.bfloat16)  14.7 us
    dot_general x1, matrix products, attend(): jnp.einsum('vphfg,vgphc->vfphc', probs, values4, preferred_element_type=j...  13.2 us
    dot_general x1, matrix products, local(): jnp.einsum('vfpd,de->vfpe', attended_tokens, w_out, preferred_element_typ...  12.3 us
    concatenate x1, other arithmetic, extended_2(): value = jnp.concatenate([before, value, after], axis=dim)  11.5 us
    slice x2, local copies, waits for them, and re-layouts, local(): query = qkv[..., :width]  11.1 us
  transfers between devices with their start and end apart: 5, of which 4 were waited for; matrix products, arithmetic and copies ran while one was open for 10% of the time, Pallas kernels for 0%

commit v1 on v0

v1 whole, which is shorter than its diff:
```python
import functools
import math

import jax
import jax.numpy as jnp
from jax import lax
from jax.experimental import pallas as pl
from jax.experimental.pallas import tpu as pltpu
from jax.sharding import PartitionSpec as P

MESH = pl.DeviceIdType.MESH
BF, F32, I32 = jnp.bfloat16, jnp.float32, jnp.int32
D = 1024
E = 2048
PATCH = 16
WINDOW = 16
REACH = 8
COUNT = 128
VIDS = 16
TMS = 8
NEG = 8
PART = COUNT // VIDS
HALF = D // 2


def nn(a, b):
    return lax.dot_general(a, b, (((1,), (0,)), ((), ())), preferred_element_type=F32)


def nt(a, b):
    return lax.dot_general(a, b, (((1,), (1,)), ((), ())), preferred_element_type=F32)


def iota(shape, dim):
    return lax.broadcasted_iota(I32, shape, dim)


def kernel(
    valid, tokens, gain, w_qkv, w_out, w_proj, offsets, negatives,
    emb_out, loss_out,
    raw, halo, wq, wk, wv, wo, wp, negs, wqvt, xn, xh, keys, keys_h, qt, vt, vt_h,
    bias, tokmean, acc, pack, got, near, own_e, count, lse_out, lse_in,
    tok_sem, w_sem, out_sem, halo_send, halo_recv, a_send, a_recv, n_send, n_recv, b_send, b_recv,
):
    vid = lax.axis_index("vid")
    tm = lax.axis_index("tm")
    left = lax.rem(tm + TMS - 1, TMS)
    right = lax.rem(tm + 1, TMS)
    peers = [lax.rem(vid + k, VIDS) for k in range(VIDS)]
    first = tm * COUNT
    length = valid[vid]

    tok_copies = [
        pltpu.make_async_copy(tokens.at[pl.ds(256 * b, 256)], raw.at[b], tok_sem.at[b])
        for b in range(8)
    ]
    w_copies = [
        pltpu.make_async_copy(src, dst, w_sem.at[i])
        for i, (src, dst) in enumerate(
            [
                (w_qkv.at[:, pl.ds(0, D)], wq),
                (w_qkv.at[:, pl.ds(2 * D, D)], wv),
                (w_qkv.at[:, pl.ds(D, D)], wk),
                (w_out, wo),
                (w_proj, wp),
                (negatives.at[:, pl.ds(pl.multiple_of(PART * vid, PART), PART), :], negs),
            ]
        )
    ]
    barrier = pltpu.get_barrier_semaphore()
    for peer in peers[1:]:
        pl.semaphore_signal(barrier, inc=1, device_id={"vid": peer}, device_id_type=MESH)
    for peer in (left, right):
        pl.semaphore_signal(barrier, inc=1, device_id={"tm": peer}, device_id_type=MESH)
    w_copies[0].start()
    tok_copies[0].start()
    w_copies[1].start()
    for copy in tok_copies[1:]:
        copy.start()
    for copy in w_copies[2:]:
        copy.start()
    pl.semaphore_wait(barrier, VIDS + 1)

    halo_copies = [
        pltpu.make_async_remote_copy(
            src_ref=tokens.at[pl.ds(256 * 7, 256)], dst_ref=halo.at[0],
            send_sem=halo_send.at[0], recv_sem=halo_recv.at[0],
            device_id={"tm": right}, device_id_type=MESH,
        ),
        pltpu.make_async_remote_copy(
            src_ref=tokens.at[pl.ds(0, 256)], dst_ref=halo.at[1],
            send_sem=halo_send.at[1], recv_sem=halo_recv.at[1],
            device_id={"tm": left}, device_id_type=MESH,
        ),
    ]
    for copy in halo_copies:
        copy.start()

    r0, r1 = iota((256, 256), 0), iota((256, 256), 1)
    perm = (r1 == (r0 % 16) * 16 + r0 // 16).astype(F32).astype(BF)
    eye = (r0 == r1).astype(F32).astype(BF)

    g0, f0 = iota((160, COUNT), 0), iota((160, COUNT), 1)
    frame = jnp.where(g0 < COUNT, g0, jnp.where(g0 < COUNT + WINDOW, g0 - COUNT - WINDOW, g0 - WINDOW))
    glob = frame + first
    ok = (jnp.abs(frame - f0) <= WINDOW) & (glob >= 0) & (glob < TMS * COUNT)
    ok = ok & ((glob < length) | (frame == f0))
    bias[...] = jnp.where(ok, 0.0, -1e30)

    w_copies[0].wait()

    def flip(src, base, scale):
        def body(i, carry):
            a = pl.multiple_of((i // 4) * 256, 256)
            b = pl.multiple_of((i % 4) * 256, 256)
            block = nt(eye, src[pl.ds(b, 256), pl.ds(a, 256)])
            wqvt[pl.ds(base + a, 256), pl.ds(b, 256)] = block.astype(BF)
            return carry
        lax.fori_loop(0, 16, body, 0)

    flip(wq, 0, 1.0)
    w_copies[1].wait()
    flip(wv, D, 1.0)

    def normed(block):
        x = nn(perm, block)
        ms = jnp.mean(x * x, axis=1, keepdims=True)
        return x, (x * lax.rsqrt(ms + 1e-5) * gain[...]).astype(BF)

    for b in range(8):
        tok_copies[b].wait()

    def norm_block(b, carry):
        x, y = normed(raw[b])
        rows = pl.ds(pl.multiple_of(16 * b, 16), 16)
        xn[:, rows, :] = y.reshape(PATCH, 16, D)
        tokmean[rows, :] = jnp.sum(x.reshape(PATCH, 16, D), axis=0) * (1.0 / PATCH)
        return carry

    lax.fori_loop(0, 8, norm_block, 0)

    w_copies[2].wait()
    scale = math.log2(math.e) / 8.0

    def project(i, carry):
        x2 = xn[pl.ds(2 * i, 2)].reshape(256, D)
        keys[pl.ds(2 * i, 2)] = nn(x2, wk[...]).astype(BF).reshape(2, COUNT, D)
        for c in range(2):
            r = nt(wqvt[512 * c:512 * c + 512], x2) * scale
            qt[2 * i, pl.ds(512 * c, 512), :] = r[:, :COUNT].astype(BF)
            qt[2 * i + 1, pl.ds(512 * c, 512), :] = r[:, COUNT:].astype(BF)
        for c in range(2):
            r = nt(wqvt[D + 512 * c:D + 512 * c + 512], x2)
            vt[2 * i, pl.ds(512 * c, 512), :] = r[:, :COUNT].astype(BF)
            vt[2 * i + 1, pl.ds(512 * c, 512), :] = r[:, COUNT:].astype(BF)
        return carry

    lax.fori_loop(0, 8, project, 0)

    for s in range(2):
        halo_copies[s].wait_recv()
        _, y = normed(halo[s])
        xh[:, 16 * s:16 * s + 16, :] = y.reshape(PATCH, 16, D)
    flat = xh[...].reshape(2 * 256, D)
    keys_h[...] = nn(flat, wk[...]).astype(BF).reshape(PATCH, 32, D)

    def project_h(c, carry):
        rows = pl.ds(pl.multiple_of(256 * c, 256), 256)
        r = nt(wqvt[pl.ds(pl.multiple_of(D + 256 * c, 256), 256)], xh[...].reshape(512, D)).astype(BF)
        for g in range(4):
            vt_h[g, rows, :] = r[:, 128 * g:128 * g + 128]
        return carry

    lax.fori_loop(0, 4, project_h, 0)

    acc[...] = jnp.zeros_like(acc)
    ones = jnp.ones((16, 256), BF)

    def attend(it, carry):
        g = it // 8
        cols = pl.ds(pl.multiple_of((it % 8) * 128, 128), 128)
        sums = [jnp.zeros((64, COUNT), F32)] * 2
        zq = jnp.zeros((64, COUNT), BF)
        zh = jnp.zeros((32, COUNT), BF)
        for q in range(4):
            p = 4 * g + q
            k = jnp.concatenate([keys[p, :, cols], keys_h[p, :, cols]], axis=0)
            ql = qt[p, cols, :]
            qbd = jnp.concatenate(
                [jnp.concatenate([ql[:64], zq], axis=1), jnp.concatenate([zq, ql[64:]], axis=1)], axis=0
            )
            st = nn(k, qbd)
            v = jnp.concatenate([vt[p, cols, :], vt_h[g, cols, :]], axis=1)
            for h in range(2):
                s = st[:, 128 * h:128 * h + 128] + bias[...]
                e = jnp.exp2(s - jnp.max(s, axis=0, keepdims=True)).astype(BF)
                e = jnp.concatenate([e[:COUNT]] + [zh] * q + [e[COUNT:]] + [zh] * (3 - q), axis=0)
                o = nn(jnp.concatenate([v[64 * h:64 * h + 64], ones], axis=0), e)
                sums[h] = sums[h] + o[:64] * (1.0 / o[64:65])
        acc[cols, :] += jnp.concatenate(sums, axis=0)
        return carry

    lax.fori_loop(0, 32, attend, 0)

    w_copies[3].wait()
    att = jnp.transpose(acc[...] * (1.0 / PATCH)).astype(BF)
    pooled = tokmean[...] + nn(att, wo[...])
    blocks = pooled.reshape(VIDS, PART, D)
    pack[...] = jnp.concatenate([blocks[:, :, :HALF], blocks[:, :, HALF:]], axis=1).astype(BF)

    pooled_copies = [
        pltpu.make_async_remote_copy(
            src_ref=pack.at[peers[k]], dst_ref=got.at[vid],
            send_sem=a_send.at[k], recv_sem=a_recv.at[k],
            device_id={"vid": peers[k]}, device_id_type=MESH,
        )
        for k in range(1, VIDS)
    ]
    near_copies = [
        pltpu.make_async_remote_copy(
            src_ref=pack.at[VIDS - 1], dst_ref=near.at[0],
            send_sem=n_send.at[0], recv_sem=n_recv.at[0],
            device_id={"tm": right}, device_id_type=MESH,
        ),
        pltpu.make_async_remote_copy(
            src_ref=pack.at[0], dst_ref=near.at[1],
            send_sem=n_send.at[1], recv_sem=n_recv.at[1],
            device_id={"tm": left}, device_id_type=MESH,
        ),
    ]
    for copy in pooled_copies + near_copies:
        copy.start()
    got[vid] = pack[vid]

    w_copies[4].wait()
    own_e[...] = nn(pooled.astype(BF), wp[...]).astype(BF)
    out_copy = pltpu.make_async_copy(own_e, emb_out, out_sem)
    out_copy.start()

    w_copies[5].wait()
    lane = iota((COUNT, COUNT), 1)
    row = iota((COUNT, COUNT), 0)
    ids = negs[...].reshape(COUNT, NEG)
    times = jnp.zeros((COUNT, COUNT), F32)
    for k in range(NEG):
        times += (ids[:, k:k + 1] * PART + row % PART == lane).astype(F32)
    count[...] = times

    e = own_e[...]
    near_own = nt(e, e)

    for copy in near_copies + pooled_copies:
        copy.wait_recv()
    seen = jnp.concatenate([got[...], near[...]], axis=0).astype(F32)
    seen = jnp.concatenate([seen[:, :PART], seen[:, PART:]], axis=2)
    seen = seen.reshape((VIDS + 2) * PART, D).astype(BF)
    all_e = nn(seen, wp[...]).astype(BF)
    factor = 8.0 / math.sqrt(E)
    gram = nt(all_e[:COUNT], all_e[:COUNT]) * factor

    frame_here = first + PART * vid + lane % PART
    other = jnp.zeros((COUNT, COUNT), I32)
    for m in range(VIDS):
        other = jnp.where(lane // PART == m, valid[m], other)
    times = count[...]
    neg = jnp.where(frame_here < other, gram, -1e30)
    top = jnp.max(jnp.where(times > 0, neg, -3e38), axis=1, keepdims=True)
    some = jnp.sum(jnp.where(times > 0, times * jnp.exp(jnp.minimum(neg - top, 0.0)), 0.0), axis=1, keepdims=True)
    lse = top + jnp.log(some)
    lse_out[...] = jnp.broadcast_to(lse, (COUNT, 128)).reshape(VIDS, PART, 128)

    back_copies = [
        pltpu.make_async_remote_copy(
            src_ref=lse_out.at[peers[k]], dst_ref=lse_in.at[vid],
            send_sem=b_send.at[k], recv_sem=b_recv.at[k],
            device_id={"vid": peers[k]}, device_id_type=MESH,
        )
        for k in range(1, VIDS)
    ]
    for copy in back_copies:
        copy.start()
    lse_in[vid] = lse_out[vid]

    near_e = nt(all_e[COUNT:], e)
    scores = jnp.concatenate([near_e[:REACH], near_own, near_e[REACH:]], axis=0)
    off = offsets[...]
    here = first + iota((1, COUNT), 1)
    ahead = here + off
    inside = (ahead >= 0) & (ahead < length)
    slot = jnp.where(inside, ahead, here - off) - first + REACH
    pick = iota((COUNT + 2 * REACH, COUNT), 0) == slot
    pos = jnp.sum(jnp.where(pick, scores, 0.0), axis=0, keepdims=True) * factor

    for copy in back_copies:
        copy.wait_recv()
    back = lse_in[...].reshape(COUNT, 128)
    lse_neg = jnp.sum(jnp.where(row == lane, back, 0.0), axis=0, keepdims=True)
    peak = jnp.maximum(pos, lse_neg)
    total = peak + jnp.log(jnp.exp(pos - peak) + jnp.exp(lse_neg - peak))
    loss_out[...] = jnp.where(here < length, total - pos, 0.0)

    for copy in halo_copies + pooled_copies + near_copies + back_copies:
        copy.wait_send()
    out_copy.wait()


def local(tokens, norm_gain, w_qkv, w_out, w_proj, offsets, negatives, valid):
    anywhere = pl.BlockSpec(memory_space=pl.ANY)
    vmem = pl.BlockSpec(memory_space=pltpu.VMEM)
    dma = pltpu.SemaphoreType.DMA
    emb, losses = pl.pallas_call(
        kernel,
        out_shape=(
            jax.ShapeDtypeStruct((COUNT, E), BF),
            jax.ShapeDtypeStruct((1, COUNT), F32),
        ),
        in_specs=[
            pl.BlockSpec(memory_space=pltpu.SMEM), anywhere, vmem, anywhere, anywhere, anywhere, vmem, anywhere,
        ],
        out_specs=(anywhere, vmem),
        scratch_shapes=[
            pltpu.VMEM((8, 256, D), BF),
            pltpu.VMEM((2, 256, D), BF),
            pltpu.VMEM((D, D), BF),
            pltpu.VMEM((D, D), BF),
            pltpu.VMEM((D, D), BF),
            pltpu.VMEM((D, D), BF),
            pltpu.VMEM((D, E), BF),
            pltpu.VMEM((VIDS, PART, NEG), I32),
            pltpu.VMEM((2 * D, D), BF),
            pltpu.VMEM((PATCH, COUNT, D), BF),
            pltpu.VMEM((PATCH, 32, D), BF),
            pltpu.VMEM((PATCH, COUNT, D), BF),
            pltpu.VMEM((PATCH, 32, D), BF),
            pltpu.VMEM((PATCH, D, COUNT), BF),
            pltpu.VMEM((PATCH, D, COUNT), BF),
            pltpu.VMEM((4, D, 128), BF),
            pltpu.VMEM((160, COUNT), F32),
            pltpu.VMEM((COUNT, D), F32),
            pltpu.VMEM((D, COUNT), F32),
            pltpu.VMEM((VIDS, 16, HALF), BF),
            pltpu.VMEM((VIDS, 16, HALF), BF),
            pltpu.VMEM((2, 16, HALF), BF),
            pltpu.VMEM((COUNT, E), BF),
            pltpu.VMEM((COUNT, COUNT), F32),
            pltpu.VMEM((VIDS, PART, 128), F32),
            pltpu.VMEM((VIDS, PART, 128), F32),
            dma((8,)), dma((6,)), dma, dma((2,)), dma((2,)), dma((VIDS,)), dma((VIDS,)),
            dma((2,)), dma((2,)), dma((VIDS,)), dma((VIDS,)),
        ],
        compiler_params=pltpu.CompilerParams(
            collective_id=0, has_side_effects=True, vmem_limit_bytes=60 * 1024 * 1024
        ),
    )(
        valid,
        tokens.reshape(COUNT * PATCH, D),
        norm_gain.reshape(1, D),
        w_qkv,
        w_out,
        w_proj,
        offsets,
        negatives,
    )
    return emb.reshape(1, COUNT, E), losses


def solution(mesh):
    placed = (
        P("vid", "tm", None, None),
        P(),
        P(),
        P(),
        P(),
        P("vid", "tm"),
        P(None, "tm", None),
        P(),
    )
    return jax.shard_map(
        local,
        mesh=mesh,
        in_specs=placed,
        out_specs=(P("vid", "tm", None), P("vid", "tm")),
        check_vma=False,
    )
```

time: 254 us -> 80.8 us (0.32)
  matrix products: 79.4 us -> 0 us
  Pallas kernels: 0 us -> 74.7 us
  waiting for transfers between devices: 74.6 us -> 0 us
  local copies, waits for them, and re-layouts: 56.1 us -> 5.23 us
  other arithmetic: 18.7 us -> 0 us
  between operations: 14.2 us -> 0.64 us
  starting transfers between devices: 9.66 us -> 0 us
    pallas_call x0 -> x1, Pallas kernels: none -> 74.7 us  [local(): pl.pallas_call(kernel, out_shape=(jax.ShapeDtypeStruct((COUNT, E), BF), j...]
    all_gather x1 -> x0, waiting for transfers between devices: 67.5 us -> none  [local(): token_piece = lax.all_gather(embeddings, 'vid', axis=0, tiled=True)]
    dot_general x6 -> x0, matrix products: 64.7 us -> none  [the longest x1 27.8 us: local(): jnp.einsum('vfpd,de->vfpe', normed, w_qkv, preferred_element_type=jnp.flo...]
    slice x6 -> x0, local copies, waits for them, and re-layouts: 33.3 us -> none  [the longest x2 11.1 us: local(): query = qkv[..., :width]]
    another operation x2 -> x0, local copies, waits for them, and re-layouts: 21.4 us -> none
    sub x1 -> x0, matrix products: 14.7 us -> none  [attend(): probs = jax.nn.softmax(scores, axis=-1).astype(jnp.bfloat16)]
    concatenate x1 -> x0, other arithmetic: 11.5 us -> none  [extended_2(): value = jnp.concatenate([before, value, after], axis=dim)]
    ppermute x4 -> x0, starting transfers between devices: 9.62 us -> none  [the longest x2 7.04 us: extended_2(): before = lax.ppermute(last, axis, up)]
  transfers between devices with their start and end apart: 5 -> 0, of which waited for: 4 -> 0; matrix products, arithmetic and copies ran while one was open for 10% -> 0% of each run, Pallas kernels for 0% -> 0%
where the time goes in v1:
time: 80.8 us; the launch traced here: 80.5 us
  Pallas kernels  74.7 us (92%)
  local copies, waits for them, and re-layouts  5.23 us (6%)
    pallas_call x1, Pallas kernels, local(): pl.pallas_call(kernel, out_shape=(jax.ShapeDtypeStruct((COUNT, E), BF), j...  74.7 us
    unnamed x3, local copies, waits for them, and re-layouts  5.23 us

profile of v1, /device:TPU:1, one launch (start us, length us, event | category | flops | bytes accessed | tf_op | source)
XLA Modules:
  0.0 80.5 jit_solution(11083916341695399827)
XLA Ops:
  0.6 2.2 %copy.10.negatives = s32[16,128,8]{2,1,0:T(8,128)} copy(s32[16,128,8]{1,2,0:T(8,128)} %param.14) | data formatting | bytes 131072 | tf_op args[6]
  2.8 74.7 %shard_map.95 = (bf16[128,2048]{1,0:T(8,128)(2,1)}, f32[1,128]{1,0:T(1,128)}) custom-call(s32[16]{0:T(128)} %valid.1, bf16[2048,1024]{1,0:T(8,128)(2,1)} %bitcast.3, f32[1,1024]{1,0:T(1,128)} %bitcast.5, bf16[1024,3072]{1,0:T(8,128)(2,1)} %w_qkv.1, bf16[1024,1024]{1,0:T(8,128)(2,1)} %w_out.1, bf16[1024,2048]{1,0:T(8,128)(2,1)} %w_proj.1, s32[1,128]{1,0:T(1,128)} %offsets.1, ...), custom_call_target="tpu_custom_call" | custom-call | tf_op jit(solution)/shard_map/pallas_call | solution.py:311
  77.5 1.9 %copy.13 = bf16[1,128,2048]{2,1,0:T(8,128)(2,1)} copy(bf16[1,128,2048]{2,1,0:T(8,128)(2,1)} %bitcast.4) | data formatting | bytes 1048576
  79.4 1.2 %copy.14 = f32[1,128]{1,0:T(1,128)} copy(f32[1,128]{1,0:T(1,128)} %get-tuple-element.9) | data formatting | bytes 1024

commit v2 on v1

--- a/solution.py
+++ b/solution.py
@@ -38,8 +38,8 @@
 def kernel(
     valid, tokens, gain, w_qkv, w_out, w_proj, offsets, negatives,
     emb_out, loss_out,
-    raw, halo, wq, wk, wv, wo, wp, negs, wqvt, xn, xh, keys, keys_h, qt, vt, vt_h,
-    bias, tokmean, acc, pack, got, near, own_e, count, lse_out, lse_in,
+    raw, halo, wq, wk, wv, wo, negs, negt, wqvt, xn, keys, qbd, vt, y0, y1,
+    bias, st0, st1, pr0, pr1, tokmean, acc, pack, got, near, own_e, count, lse_out, lse_in,
     tok_sem, w_sem, out_sem, halo_send, halo_recv, a_send, a_recv, n_send, n_recv, b_send, b_recv,
 ):
     vid = lax.axis_index("vid")
@@ -62,8 +62,9 @@
                 (w_qkv.at[:, pl.ds(2 * D, D)], wv),
                 (w_qkv.at[:, pl.ds(D, D)], wk),
                 (w_out, wo),
-                (w_proj, wp),
-                (negatives.at[:, pl.ds(pl.multiple_of(PART * vid, PART), PART), :], negs),
+                (negatives, negs),
+                (w_proj.at[:, pl.ds(0, D)], wq),
+                (w_proj.at[:, pl.ds(D, D)], wv),
             ]
         )
     ]
@@ -77,7 +78,7 @@
     w_copies[1].start()
     for copy in tok_copies[1:]:
         copy.start()
-    for copy in w_copies[2:]:
+    for copy in w_copies[2:5]:
         copy.start()
     pl.semaphore_wait(barrier, VIDS + 1)
 
@@ -99,111 +100,192 @@
     r0, r1 = iota((256, 256), 0), iota((256, 256), 1)
     perm = (r1 == (r0 % 16) * 16 + r0 // 16).astype(F32).astype(BF)
     eye = (r0 == r1).astype(F32).astype(BF)
-
-    g0, f0 = iota((160, COUNT), 0), iota((160, COUNT), 1)
-    frame = jnp.where(g0 < COUNT, g0, jnp.where(g0 < COUNT + WINDOW, g0 - COUNT - WINDOW, g0 - WINDOW))
-    glob = frame + first
-    ok = (jnp.abs(frame - f0) <= WINDOW) & (glob >= 0) & (glob < TMS * COUNT)
-    ok = ok & ((glob < length) | (frame == f0))
-    bias[...] = jnp.where(ok, 0.0, -1e30)
+    avg = jnp.where(iota((16, 256), 0) == iota((16, 256), 1) // 16, 1.0 / PATCH, 0.0).astype(BF)
+
+    g0, f0 = iota((64, 128), 0), iota((64, 128), 1) % 32
+    for b in range(4):
+        frame = g0 + (32 * b - WINDOW)
+        query = f0 + 32 * b
+        glob = frame + first
+        ok = (jnp.abs(frame - query) <= WINDOW) & (glob >= 0) & (glob < TMS * COUNT)
+        ok = ok & ((glob < length) | (frame == query))
+        bias[b] = jnp.where(ok, 0.0, -1e30)
+    lane_block = iota((64, 128), 1) // 32
+
+    w_copies[4].wait()
+    lane = iota((COUNT, COUNT), 1)
+    row = iota((COUNT, COUNT), 0)
+    negt[...] = jnp.transpose(negs[...].reshape(VIDS * NEG, COUNT).astype(F32))
+    ids = negt[pl.ds(pl.multiple_of(PART * vid, PART), PART), :]
+    ids = jnp.concatenate([ids] * VIDS, axis=0)
+    times = jnp.zeros((COUNT, COUNT), F32)
+    for k in range(NEG):
+        one = jnp.sum(jnp.where(lane == row // PART * NEG + k, ids, 0.0), axis=1, keepdims=True)
+        times += (one * PART + (row % PART).astype(F32) == lane.astype(F32)).astype(F32)
+    count[...] = times
 
     w_copies[0].wait()
 
-    def flip(src, base, scale):
+    def flip(src, base):
         def body(i, carry):
-            a = pl.multiple_of((i // 4) * 256, 256)
-            b = pl.multiple_of((i % 4) * 256, 256)
-            block = nt(eye, src[pl.ds(b, 256), pl.ds(a, 256)])
-            wqvt[pl.ds(base + a, 256), pl.ds(b, 256)] = block.astype(BF)
+            a = pl.multiple_of(i * 256, 256)
+            for c in range(4):
+                block = nt(eye, src[256 * c:256 * c + 256, pl.ds(a, 256)])
+                wqvt[pl.ds(base + a, 256), 256 * c:256 * c + 256] = block.astype(BF)
             return carry
-        lax.fori_loop(0, 16, body, 0)
-
-    flip(wq, 0, 1.0)
+        lax.fori_loop(0, 4, body, 0)
+
+    flip(wq, 0)
     w_copies[1].wait()
-    flip(wv, D, 1.0)
-
-    def normed(block):
+    flip(wv, D)
+    w_copies[5].start()
+    w_copies[6].start()
+
+    def normed(block, rows, out):
         x = nn(perm, block)
         ms = jnp.mean(x * x, axis=1, keepdims=True)
-        return x, (x * lax.rsqrt(ms + 1e-5) * gain[...]).astype(BF)
+        y = (x * lax.rsqrt(ms + 1e-5) * gain[...]).astype(BF)
+        out[...] = y
+        xn[:, rows, :] = y.reshape(PATCH, 16, D)
+
+    def keys_of(y, rows):
+        keys[:, rows, :] = nn(y[...], wk[...]).astype(BF).reshape(PATCH, 16, D)
+
+    def rows_of(b):
+        return pl.ds(pl.multiple_of(16 * b + 16, 16), 16)
+
+    def own(b, out):
+        block = raw[b]
+        normed(block, rows_of(b), out)
+        tokmean[pl.ds(pl.multiple_of(16 * b, 16), 16), :] = nn(avg, block)
 
     for b in range(8):
         tok_copies[b].wait()
-
-    def norm_block(b, carry):
-        x, y = normed(raw[b])
-        rows = pl.ds(pl.multiple_of(16 * b, 16), 16)
-        xn[:, rows, :] = y.reshape(PATCH, 16, D)
-        tokmean[rows, :] = jnp.sum(x.reshape(PATCH, 16, D), axis=0) * (1.0 / PATCH)
-        return carry
-
-    lax.fori_loop(0, 8, norm_block, 0)
-
     w_copies[2].wait()
+    own(0, y0)
+
+    def norm_pair(i, carry):
+        own(2 * i + 1, y1)
+        keys_of(y0, rows_of(2 * i))
+        own(2 * i + 2, y0)
+        keys_of(y1, rows_of(2 * i + 1))
+        return carry
+
+    lax.fori_loop(0, 3, norm_pair, 0)
+    own(7, y1)
+    keys_of(y0, rows_of(6))
+    keys_of(y1, rows_of(7))
+
     scale = math.log2(math.e) / 8.0
 
-    def project(i, carry):
-        x2 = xn[pl.ds(2 * i, 2)].reshape(256, D)
-        keys[pl.ds(2 * i, 2)] = nn(x2, wk[...]).astype(BF).reshape(2, COUNT, D)
+    def queries(i, carry):
+        x2 = xn[pl.ds(2 * i, 2), 16:16 + COUNT, :].reshape(256, D)
         for c in range(2):
             r = nt(wqvt[512 * c:512 * c + 512], x2) * scale
-            qt[2 * i, pl.ds(512 * c, 512), :] = r[:, :COUNT].astype(BF)
-            qt[2 * i + 1, pl.ds(512 * c, 512), :] = r[:, COUNT:].astype(BF)
+            for u in range(2):
+                for n in range(8):
+                    j, h = 2 * c + n // 4, n % 4
+                    part = r[64 * n:64 * n + 64, COUNT * u:COUNT * u + COUNT]
+                    if h:
+                        part = pltpu.roll(part, 32 * h, 1)
+                    part = part.astype(BF)
+                    for b in range(4):
+                        masked = jnp.where(lane_block == (b + h) % 4, part, 0.0)
+                        qbd[2 * i + u, j, b, 64 * h:64 * h + 64, :] = masked.astype(BF)
+        return carry
+
+    lax.fori_loop(0, 8, queries, 0)
+
+    def values(ga, ra, gb, rb):
+        xa = xn[pl.ds(4 * ga, 4), 32 * ra:32 * ra + 32, :].reshape(128, D)
+        xb = xn[pl.ds(4 * gb, 4), 32 * rb:32 * rb + 32, :].reshape(128, D)
+        x2 = jnp.concatenate([xa, xb], axis=0)
         for c in range(2):
-            r = nt(wqvt[D + 512 * c:D + 512 * c + 512], x2)
-            vt[2 * i, pl.ds(512 * c, 512), :] = r[:, :COUNT].astype(BF)
-            vt[2 * i + 1, pl.ds(512 * c, 512), :] = r[:, COUNT:].astype(BF)
-        return carry
-
-    lax.fori_loop(0, 8, project, 0)
-
-    for s in range(2):
-        halo_copies[s].wait_recv()
-        _, y = normed(halo[s])
-        xh[:, 16 * s:16 * s + 16, :] = y.reshape(PATCH, 16, D)
-    flat = xh[...].reshape(2 * 256, D)
-    keys_h[...] = nn(flat, wk[...]).astype(BF).reshape(PATCH, 32, D)
-
-    def project_h(c, carry):
-        rows = pl.ds(pl.multiple_of(256 * c, 256), 256)
-        r = nt(wqvt[pl.ds(pl.multiple_of(D + 256 * c, 256), 256)], xh[...].reshape(512, D)).astype(BF)
-        for g in range(4):
-            vt_h[g, rows, :] = r[:, 128 * g:128 * g + 128]
-        return carry
-
-    lax.fori_loop(0, 4, project_h, 0)
+            r = nt(wqvt[D + 512 * c:D + 512 * c + 512], x2).astype(BF)
+            vt[ga, 512 * c:512 * c + 512, 128 * ra:128 * ra + 128] = r[:, :128]
+            vt[gb, 512 * c:512 * c + 512, 128 * rb:128 * rb + 128] = r[:, 128:]
+
+    def values_inner(g, carry):
+        values(g, 1, g, 2)
+        return carry
+
+    def values_last(g, carry):
+        values(2 * g, 3, 2 * g + 1, 3)
+        return carry
+
+    lax.fori_loop(0, 4, values_inner, 0)
+    lax.fori_loop(0, 2, values_last, 0)
+
+    halo_copies[0].wait_recv()
+    normed(halo[0], pl.ds(0, 16), y0)
+    halo_copies[1].wait_recv()
+    normed(halo[1], pl.ds(16 + COUNT, 16), y1)
+    keys_of(y0, pl.ds(0, 16))
+    keys_of(y1, pl.ds(16 + COUNT, 16))
+
+    def values_outer(g, carry):
+        values(g, 0, g, 4)
+        return carry
+
+    lax.fori_loop(0, 4, values_outer, 0)
 
     acc[...] = jnp.zeros_like(acc)
-    ones = jnp.ones((16, 256), BF)
-
-    def attend(it, carry):
-        g = it // 8
-        cols = pl.ds(pl.multiple_of((it % 8) * 128, 128), 128)
-        sums = [jnp.zeros((64, COUNT), F32)] * 2
-        zq = jnp.zeros((64, COUNT), BF)
-        zh = jnp.zeros((32, COUNT), BF)
+
+    def where_is(u):
+        return u // 4, u % 4
+
+    def scores_of(u, out):
+        g, j = where_is(u)
+        cols = pl.ds(pl.multiple_of(256 * j, 256), 256)
         for q in range(4):
-            p = 4 * g + q
-            k = jnp.concatenate([keys[p, :, cols], keys_h[p, :, cols]], axis=0)
-            ql = qt[p, cols, :]
-            qbd = jnp.concatenate(
-                [jnp.concatenate([ql[:64], zq], axis=1), jnp.concatenate([zq, ql[64:]], axis=1)], axis=0
-            )
-            st = nn(k, qbd)
-            v = jnp.concatenate([vt[p, cols, :], vt_h[g, cols, :]], axis=1)
-            for h in range(2):
-                s = st[:, 128 * h:128 * h + 128] + bias[...]
-                e = jnp.exp2(s - jnp.max(s, axis=0, keepdims=True)).astype(BF)
-                e = jnp.concatenate([e[:COUNT]] + [zh] * q + [e[COUNT:]] + [zh] * (3 - q), axis=0)
-                o = nn(jnp.concatenate([v[64 * h:64 * h + 64], ones], axis=0), e)
-                sums[h] = sums[h] + o[:64] * (1.0 / o[64:65])
-        acc[cols, :] += jnp.concatenate(sums, axis=0)
-        return carry
-
-    lax.fori_loop(0, 32, attend, 0)
+            for b in range(4):
+                out[q, b] = nn(keys[4 * g + q, 32 * b:32 * b + 64, cols], qbd[4 * g + q, j, b])
+
+    def softmax_of(src, out):
+        for b in range(4):
+            mask = bias[b]
+            for q in range(4):
+                s = src[q, b] + mask
+                e = jnp.exp2(s - jnp.max(s, axis=0, keepdims=True))
+                e = (e * (1.0 / jnp.sum(e, axis=0, keepdims=True))).astype(BF)
+                out[b, 32 * q:32 * q + 32, :] = e[:32]
+                out[b, 128 + 32 * q:128 + 32 * q + 32, :] = e[32:]
+
+    def attended_of(u, probs):
+        g, j = where_is(u)
+        rows = pl.ds(pl.multiple_of(256 * j, 256), 256)
+        parts = [nn(vt[g, rows, 128 * b:128 * b + 256], probs[b]) for b in range(4)]
+        for h in range(4):
+            pick = parts[0][64 * h:64 * h + 64]
+            for b in range(1, 4):
+                pick = jnp.where(lane_block == (b + h) % 4, parts[b][64 * h:64 * h + 64], pick)
+            acc[pl.ds(pl.multiple_of(256 * j + 64 * h, 64), 64), :] += pick
+
+    scores_of(0, st0)
+    scores_of(1, st1)
+    softmax_of(st0, pr0)
+
+    def attend(i, carry):
+        u = 2 * i
+        scores_of(u + 2, st0)
+        softmax_of(st1, pr1)
+        attended_of(u, pr0)
+        scores_of(u + 3, st1)
+        softmax_of(st0, pr0)
+        attended_of(u + 1, pr1)
+        return carry
+
+    lax.fori_loop(0, 7, attend, 0)
+    softmax_of(st1, pr1)
+    attended_of(14, pr0)
+    attended_of(15, pr1)
 
     w_copies[3].wait()
-    att = jnp.transpose(acc[...] * (1.0 / PATCH)).astype(BF)
+    heads = []
+    for h in range(16):
+        part = acc[64 * h:64 * h + 64, :]
+        heads.append(pltpu.roll(part, 128 - 32 * (h % 4), 1) if h % 4 else part)
+    att = jnp.transpose(jnp.concatenate(heads, axis=0) * (1.0 / PATCH)).astype(BF)
     pooled = tokmean[...] + nn(att, wo[...])
     blocks = pooled.reshape(VIDS, PART, D)
     pack[...] = jnp.concatenate([blocks[:, :, :HALF], blocks[:, :, HALF:]], axis=1).astype(BF)
@@ -232,19 +314,13 @@
         copy.start()
     got[vid] = pack[vid]
 
-    w_copies[4].wait()
-    own_e[...] = nn(pooled.astype(BF), wp[...]).astype(BF)
+    w_copies[5].wait()
+    w_copies[6].wait()
+    mine = pooled.astype(BF)
+    own_e[:, :D] = nn(mine, wq[...]).astype(BF)
+    own_e[:, D:] = nn(mine, wv[...]).astype(BF)
     out_copy = pltpu.make_async_copy(own_e, emb_out, out_sem)
     out_copy.start()
-
-    w_copies[5].wait()
-    lane = iota((COUNT, COUNT), 1)
-    row = iota((COUNT, COUNT), 0)
-    ids = negs[...].reshape(COUNT, NEG)
-    times = jnp.zeros((COUNT, COUNT), F32)
-    for k in range(NEG):
-        times += (ids[:, k:k + 1] * PART + row % PART == lane).astype(F32)
-    count[...] = times
 
     e = own_e[...]
     near_own = nt(e, e)
@@ -254,7 +330,7 @@
     seen = jnp.concatenate([got[...], near[...]], axis=0).astype(F32)
     seen = jnp.concatenate([seen[:, :PART], seen[:, PART:]], axis=2)
     seen = seen.reshape((VIDS + 2) * PART, D).astype(BF)
-    all_e = nn(seen, wp[...]).astype(BF)
+    all_e = jnp.concatenate([nn(seen, wq[...]).astype(BF), nn(seen, wv[...]).astype(BF)], axis=1)
     factor = 8.0 / math.sqrt(E)
     gram = nt(all_e[:COUNT], all_e[:COUNT]) * factor
 
@@ -325,17 +401,20 @@
             pltpu.VMEM((D, D), BF),
             pltpu.VMEM((D, D), BF),
             pltpu.VMEM((D, D), BF),
-            pltpu.VMEM((D, E), BF),
-            pltpu.VMEM((VIDS, PART, NEG), I32),
+            pltpu.VMEM((VIDS, NEG, COUNT), I32),
+            pltpu.VMEM((COUNT, VIDS * NEG), F32),
             pltpu.VMEM((2 * D, D), BF),
-            pltpu.VMEM((PATCH, COUNT, D), BF),
-            pltpu.VMEM((PATCH, 32, D), BF),
-            pltpu.VMEM((PATCH, COUNT, D), BF),
-            pltpu.VMEM((PATCH, 32, D), BF),
-            pltpu.VMEM((PATCH, D, COUNT), BF),
-            pltpu.VMEM((PATCH, D, COUNT), BF),
-            pltpu.VMEM((4, D, 128), BF),
-            pltpu.VMEM((160, COUNT), F32),
+            pltpu.VMEM((PATCH, 160, D), BF),
+            pltpu.VMEM((PATCH, 160, D), BF),
+            pltpu.VMEM((PATCH, 4, 4, 256, 128), BF),
+            pltpu.VMEM((4, D, 640), BF),
+            pltpu.VMEM((256, D), BF),
+            pltpu.VMEM((256, D), BF),
+            pltpu.VMEM((4, 64, 128), F32),
+            pltpu.VMEM((4, 4, 64, 128), F32),
+            pltpu.VMEM((4, 4, 64, 128), F32),
+            pltpu.VMEM((4, 256, 128), BF),
+            pltpu.VMEM((4, 256, 128), BF),
             pltpu.VMEM((COUNT, D), F32),
             pltpu.VMEM((D, COUNT), F32),
             pltpu.VMEM((VIDS, 16, HALF), BF),
@@ -345,7 +424,7 @@
             pltpu.VMEM((COUNT, COUNT), F32),
             pltpu.VMEM((VIDS, PART, 128), F32),
             pltpu.VMEM((VIDS, PART, 128), F32),
-            dma((8,)), dma((6,)), dma, dma((2,)), dma((2,)), dma((VIDS,)), dma((VIDS,)),
+            dma((8,)), dma((7,)), dma, dma((2,)), dma((2,)), dma((VIDS,)), dma((VIDS,)),
             dma((2,)), dma((2,)), dma((VIDS,)), dma((VIDS,)),
         ],
         compiler_params=pltpu.CompilerParams(
@@ -359,7 +438,7 @@
         w_out,
         w_proj,
         offsets,
-        negatives,
+        jnp.swapaxes(negatives, 1, 2),
     )
     return emb.reshape(1, COUNT, E), losses
 

time: 80.8 us -> 62 us (0.77)
  Pallas kernels: 74.7 us -> 58.2 us
  local copies, waits for them, and re-layouts: 5.23 us -> 2.99 us
    pallas_call x1, Pallas kernels: 74.7 us -> 58.2 us  [local(): pl.pallas_call(kernel, out_shape=(jax.ShapeDtypeStruct((COUNT, E), BF), j...]
    unnamed x3 -> x2, local copies, waits for them, and re-layouts: 5.23 us -> 2.99 us
where the time goes in v2:
time: 62 us; the launch traced here: 61.8 us
  Pallas kernels  58.2 us (94%)
  local copies, waits for them, and re-layouts  2.99 us (5%)
  between operations  0.64 us (1%)
    pallas_call x1, Pallas kernels, local(): pl.pallas_call(kernel, out_shape=(jax.ShapeDtypeStruct((COUNT, E), BF), j...  58.2 us
    unnamed x2, local copies, waits for them, and re-layouts  2.99 us

profile of v2, /device:TPU:1, one launch (start us, length us, event | category | flops | bytes accessed | tf_op | source)
XLA Modules:
  0.0 61.8 jit_solution(7943726070750468148)
XLA Ops:
  0.6 58.2 %shard_map.95 = (bf16[128,2048]{1,0:T(8,128)(2,1)}, f32[1,128]{1,0:T(1,128)}) custom-call(s32[16]{0:T(128)} %valid.1, bf16[2048,1024]{1,0:T(8,128)(2,1)} %bitcast.4, f32[1,1024]{1,0:T(1,128)} %bitcast.7, bf16[1024,3072]{1,0:T(8,128)(2,1)} %w_qkv.1, bf16[1024,1024]{1,0:T(8,128)(2,1)} %w_out.1, bf16[1024,2048]{1,0:T(8,128)(2,1)} %w_proj.1, s32[1,128]{1,0:T(1,128)} %offsets.1, ...), custom_call_target="tpu_custom_call" | custom-call | tf_op jit(solution)/shard_map/pallas_call | solution.py:387
  58.8 1.9 %copy.12 = bf16[1,128,2048]{2,1,0:T(8,128)(2,1)} copy(bf16[1,128,2048]{2,1,0:T(8,128)(2,1)} %bitcast.5) | data formatting | bytes 1048576
  60.7 1.1 %copy.13 = f32[1,128]{1,0:T(1,128)} copy(f32[1,128]{1,0:T(1,128)} %get-tuple-element.9) | data formatting | bytes 1024

commit v3 on v2

--- a/solution.py
+++ b/solution.py
@@ -1,4 +1,4 @@
-import functools
+import itertools
 import math
 
 import jax
@@ -38,15 +38,16 @@
 def kernel(
     valid, tokens, gain, w_qkv, w_out, w_proj, offsets, negatives,
     emb_out, loss_out,
-    raw, halo, wq, wk, wv, wo, negs, negt, wqvt, xn, keys, qbd, vt, y0, y1,
-    bias, st0, st1, pr0, pr1, tokmean, acc, pack, got, near, own_e, count, lse_out, lse_in,
-    tok_sem, w_sem, out_sem, halo_send, halo_recv, a_send, a_recv, n_send, n_recv, b_send, b_recv,
+    raw, halo, wq, wk, wv, wo, negs, negt, wqvt, xn, keys, qt, vt, y0, y1,
+    bias, st0, st1, pr0, pr1, tokmean, acc, pack, got, near, own_e, count_out, count, lse_out, lse_in,
+    tok_sem, w_sem, out_sem, halo_send, halo_recv, a_send, a_recv, n_send, n_recv, b_send, b_recv, c_send, c_recv,
 ):
     vid = lax.axis_index("vid")
     tm = lax.axis_index("tm")
     left = lax.rem(tm + TMS - 1, TMS)
     right = lax.rem(tm + 1, TMS)
-    peers = [lax.rem(vid + k, VIDS) for k in range(VIDS)]
+    across = lax.rem(tm + TMS // 2, TMS)
+    peers = [{"vid": lax.rem(vid + k, VIDS), "tm": across} for k in range(VIDS)]
     first = tm * COUNT
     length = valid[vid]
 
@@ -69,8 +70,8 @@
         )
     ]
     barrier = pltpu.get_barrier_semaphore()
-    for peer in peers[1:]:
-        pl.semaphore_signal(barrier, inc=1, device_id={"vid": peer}, device_id_type=MESH)
+    for peer in peers:
+        pl.semaphore_signal(barrier, inc=1, device_id=peer, device_id_type=MESH)
     for peer in (left, right):
         pl.semaphore_signal(barrier, inc=1, device_id={"tm": peer}, device_id_type=MESH)
     w_copies[0].start()
@@ -80,23 +81,6 @@
         copy.start()
     for copy in w_copies[2:5]:
         copy.start()
-    pl.semaphore_wait(barrier, VIDS + 1)
-
-    halo_copies = [
-        pltpu.make_async_remote_copy(
-            src_ref=tokens.at[pl.ds(256 * 7, 256)], dst_ref=halo.at[0],
-            send_sem=halo_send.at[0], recv_sem=halo_recv.at[0],
-            device_id={"tm": right}, device_id_type=MESH,
-        ),
-        pltpu.make_async_remote_copy(
-            src_ref=tokens.at[pl.ds(0, 256)], dst_ref=halo.at[1],
-            send_sem=halo_send.at[1], recv_sem=halo_recv.at[1],
-            device_id={"tm": left}, device_id_type=MESH,
-        ),
-    ]
-    for copy in halo_copies:
-        copy.start()
-
     r0, r1 = iota((256, 256), 0), iota((256, 256), 1)
     perm = (r1 == (r0 % 16) * 16 + r0 // 16).astype(F32).astype(BF)
     eye = (r0 == r1).astype(F32).astype(BF)
@@ -122,7 +106,7 @@
     for k in range(NEG):
         one = jnp.sum(jnp.where(lane == row // PART * NEG + k, ids, 0.0), axis=1, keepdims=True)
         times += (one * PART + (row % PART).astype(F32) == lane.astype(F32)).astype(F32)
-    count[...] = times
+    count_out[...] = times
 
     w_copies[0].wait()
 
@@ -141,40 +125,67 @@
     w_copies[5].start()
     w_copies[6].start()
 
-    def normed(block, rows, out):
-        x = nn(perm, block)
-        ms = jnp.mean(x * x, axis=1, keepdims=True)
-        y = (x * lax.rsqrt(ms + 1e-5) * gain[...]).astype(BF)
-        out[...] = y
-        xn[:, rows, :] = y.reshape(PATCH, 16, D)
-
-    def keys_of(y, rows):
-        keys[:, rows, :] = nn(y[...], wk[...]).astype(BF).reshape(PATCH, 16, D)
+    pl.semaphore_wait(barrier, VIDS + 2)
+
+    halo_copies = [
+        pltpu.make_async_remote_copy(
+            src_ref=tokens.at[pl.ds(256 * 7, 256)], dst_ref=halo.at[0],
+            send_sem=halo_send.at[0], recv_sem=halo_recv.at[0],
+            device_id={"tm": right}, device_id_type=MESH,
+        ),
+        pltpu.make_async_remote_copy(
+            src_ref=tokens.at[pl.ds(0, 256)], dst_ref=halo.at[1],
+            send_sem=halo_send.at[1], recv_sem=halo_recv.at[1],
+            device_id={"tm": left}, device_id_type=MESH,
+        ),
+    ]
+    for copy in halo_copies:
+        copy.start()
+
+    count_copy = pltpu.make_async_remote_copy(
+        src_ref=count_out, dst_ref=count, send_sem=c_send, recv_sem=c_recv, device_id=peers[0], device_id_type=MESH,
+    )
+    count_copy.start()
+
+    def normed(block, out, rows=(0, 1, 2, 3)):
+        for c in rows:
+            for n in range(4):
+                at = 64 * c + 16 * n
+                x = block[at:at + 16, :].astype(F32)
+                mean = jnp.sum(x * x, axis=1, keepdims=True) * (1.0 / D)
+                out[at:at + 16, :] = (x * lax.rsqrt(mean + 1e-5) * gain[...]).astype(BF)
+            yield
+
+    def permuted(y, rows):
+        for c in range(4):
+            part = nn(perm, y[:, 256 * c:256 * c + 256]).astype(BF)
+            xn[:, rows, 256 * c:256 * c + 256] = part.reshape(PATCH, 16, 256)
+            yield
+
+    def averaged(b):
+        tokmean[pl.ds(pl.multiple_of(16 * b, 16), 16), :] = nn(avg, raw[b])
+        yield
 
     def rows_of(b):
         return pl.ds(pl.multiple_of(16 * b + 16, 16), 16)
 
-    def own(b, out):
-        block = raw[b]
-        normed(block, rows_of(b), out)
-        tokmean[pl.ds(pl.multiple_of(16 * b, 16), 16), :] = nn(avg, block)
+    def weave(*jobs):
+        for _ in itertools.zip_longest(*jobs):
+            pass
 
     for b in range(8):
         tok_copies[b].wait()
-    w_copies[2].wait()
-    own(0, y0)
+    weave(normed(raw.at[0], y0))
 
     def norm_pair(i, carry):
-        own(2 * i + 1, y1)
-        keys_of(y0, rows_of(2 * i))
-        own(2 * i + 2, y0)
-        keys_of(y1, rows_of(2 * i + 1))
+        b = 2 * i
+        weave(permuted(y0, rows_of(b)), normed(raw.at[b + 1], y1), averaged(b))
+        weave(permuted(y1, rows_of(b + 1)), normed(raw.at[b + 2], y0), averaged(b + 1))
         return carry
 
     lax.fori_loop(0, 3, norm_pair, 0)
-    own(7, y1)
-    keys_of(y0, rows_of(6))
-    keys_of(y1, rows_of(7))
+    weave(permuted(y0, rows_of(6)), normed(raw.at[7], y1), averaged(6))
+    weave(permuted(y1, rows_of(7)), averaged(7))
 
     scale = math.log2(math.e) / 8.0
 
@@ -184,14 +195,10 @@
             r = nt(wqvt[512 * c:512 * c + 512], x2) * scale
             for u in range(2):
                 for n in range(8):
-                    j, h = 2 * c + n // 4, n % 4
                     part = r[64 * n:64 * n + 64, COUNT * u:COUNT * u + COUNT]
-                    if h:
-                        part = pltpu.roll(part, 32 * h, 1)
-                    part = part.astype(BF)
-                    for b in range(4):
-                        masked = jnp.where(lane_block == (b + h) % 4, part, 0.0)
-                        qbd[2 * i + u, j, b, 64 * h:64 * h + 64, :] = masked.astype(BF)
+                    if n % 4:
+                        part = pltpu.roll(part, 32 * (n % 4), 1)
+                    qt[2 * i + u, 512 * c + 64 * n:512 * c + 64 * n + 64, :] = part.astype(BF)
         return carry
 
     lax.fori_loop(0, 8, queries, 0)
@@ -217,11 +224,20 @@
     lax.fori_loop(0, 2, values_last, 0)
 
     halo_copies[0].wait_recv()
-    normed(halo[0], pl.ds(0, 16), y0)
     halo_copies[1].wait_recv()
-    normed(halo[1], pl.ds(16 + COUNT, 16), y1)
-    keys_of(y0, pl.ds(0, 16))
-    keys_of(y1, pl.ds(16 + COUNT, 16))
+    weave(normed(halo.at[0], y0))
+    weave(permuted(y0, pl.ds(0, 16)), normed(halo.at[1], y1))
+    weave(permuted(y1, pl.ds(16 + COUNT, 16)))
+
+    w_copies[2].wait()
+
+    def project_keys(i, carry):
+        rows = pl.ds(pl.multiple_of(512 * i, 512), 512)
+        for c in range(2):
+            keys[rows, 512 * c:512 * c + 512] = nn(xn.reshape(PATCH * 160, D)[rows, :], wk[:, 512 * c:512 * c + 512]).astype(BF)
+        return carry
+
+    lax.fori_loop(0, 5, project_keys, 0)
 
     def values_outer(g, carry):
         values(g, 0, g, 4)
@@ -232,53 +248,62 @@
     acc[...] = jnp.zeros_like(acc)
 
     def where_is(u):
-        return u // 4, u % 4
+        return u // 2, pl.ds(pl.multiple_of(512 * (u % 2), 512), 512)
+
+    diagonal = [jnp.concatenate([lane_block == (b + h) % 4 for h in range(4)] * 2, axis=0) for b in range(4)]
 
     def scores_of(u, out):
-        g, j = where_is(u)
-        cols = pl.ds(pl.multiple_of(256 * j, 256), 256)
+        g, cols = where_is(u)
+        for q in range(4):
+            p = 4 * g + q
+            for b in range(4):
+                q8 = qt[p, cols, :]
+                q8 = jnp.where(diagonal[b], q8, jnp.zeros_like(q8))
+                k8 = keys[pl.ds(pl.multiple_of(160 * p + 32 * b, 32), 64), cols]
+                r = nn(
+                    jnp.concatenate([k8[:, :256], k8[:, 256:]], axis=0),
+                    jnp.concatenate([q8[:256], q8[256:]], axis=1),
+                )
+                out[q, b, :, :128] = r[:64, :128]
+                out[q, b, :, 128:] = r[64:, 128:]
+                yield
+
+    def softmax_of(src, out):
         for q in range(4):
             for b in range(4):
-                out[q, b] = nn(keys[4 * g + q, 32 * b:32 * b + 64, cols], qbd[4 * g + q, j, b])
-
-    def softmax_of(src, out):
+                for j in range(2):
+                    s = src[q, b, :, 128 * j:128 * j + 128] + bias[b]
+                    e = jnp.exp2(s - jnp.max(s, axis=0, keepdims=True))
+                    e = (e * (1.0 / jnp.sum(e, axis=0, keepdims=True))).astype(BF)
+                    out[b, 32 * q:32 * q + 32, 128 * j:128 * j + 128] = e[:32]
+                    out[b, 128 + 32 * q:128 + 32 * q + 32, 128 * j:128 * j + 128] = e[32:]
+                yield
+
+    def attended_of(u, probs):
+        g, rows = where_is(u)
         for b in range(4):
-            mask = bias[b]
-            for q in range(4):
-                s = src[q, b] + mask
-                e = jnp.exp2(s - jnp.max(s, axis=0, keepdims=True))
-                e = (e * (1.0 / jnp.sum(e, axis=0, keepdims=True))).astype(BF)
-                out[b, 32 * q:32 * q + 32, :] = e[:32]
-                out[b, 128 + 32 * q:128 + 32 * q + 32, :] = e[32:]
-
-    def attended_of(u, probs):
-        g, j = where_is(u)
-        rows = pl.ds(pl.multiple_of(256 * j, 256), 256)
-        parts = [nn(vt[g, rows, 128 * b:128 * b + 256], probs[b]) for b in range(4)]
-        for h in range(4):
-            pick = parts[0][64 * h:64 * h + 64]
-            for b in range(1, 4):
-                pick = jnp.where(lane_block == (b + h) % 4, parts[b][64 * h:64 * h + 64], pick)
-            acc[pl.ds(pl.multiple_of(256 * j + 64 * h, 64), 64), :] += pick
-
-    scores_of(0, st0)
-    scores_of(1, st1)
-    softmax_of(st0, pr0)
+            r = nn(vt[g, rows, 128 * b:128 * b + 256], probs[b])
+            for j in range(2):
+                for h in range(4):
+                    at = 256 * j + 64 * h
+                    part = r[at:at + 64, 128 * j:128 * j + 128]
+                    where = pl.ds(pl.multiple_of(512 * (u % 2) + at, 64), 64)
+                    acc[where, :] += jnp.where(lane_block == (b + h) % 4, part, 0.0)
+            for _ in range(4):
+                yield
+
+    weave(scores_of(0, st0))
+    weave(scores_of(1, st1), softmax_of(st0, pr0))
 
     def attend(i, carry):
         u = 2 * i
-        scores_of(u + 2, st0)
-        softmax_of(st1, pr1)
-        attended_of(u, pr0)
-        scores_of(u + 3, st1)
-        softmax_of(st0, pr0)
-        attended_of(u + 1, pr1)
-        return carry
-
-    lax.fori_loop(0, 7, attend, 0)
-    softmax_of(st1, pr1)
-    attended_of(14, pr0)
-    attended_of(15, pr1)
+        weave(scores_of(u + 2, st0), softmax_of(st1, pr1), attended_of(u, pr0))
+        weave(scores_of(u + 3, st1), softmax_of(st0, pr0), attended_of(u + 1, pr1))
+        return carry
+
+    lax.fori_loop(0, 3, attend, 0)
+    weave(softmax_of(st1, pr1), attended_of(6, pr0))
+    weave(attended_of(7, pr1))
 
     w_copies[3].wait()
     heads = []
@@ -292,11 +317,11 @@
 
     pooled_copies = [
         pltpu.make_async_remote_copy(
-            src_ref=pack.at[peers[k]], dst_ref=got.at[vid],
-            send_sem=a_send.at[k], recv_sem=a_recv.at[k],
-            device_id={"vid": peers[k]}, device_id_type=MESH,
+            src_ref=pack.at[peers[k]["vid"]], dst_ref=got.at[vid],
+            send_sem=a_send, recv_sem=a_recv,
+            device_id=peers[k], device_id_type=MESH,
         )
-        for k in range(1, VIDS)
+        for k in range(VIDS)
     ]
     near_copies = [
         pltpu.make_async_remote_copy(
@@ -312,7 +337,6 @@
     ]
     for copy in pooled_copies + near_copies:
         copy.start()
-    got[vid] = pack[vid]
 
     w_copies[5].wait()
     w_copies[6].wait()
@@ -325,8 +349,9 @@
     e = own_e[...]
     near_own = nt(e, e)
 
-    for copy in near_copies + pooled_copies:
+    for copy in near_copies:
         copy.wait_recv()
+    pltpu.make_async_copy(got, got, a_recv).wait()
     seen = jnp.concatenate([got[...], near[...]], axis=0).astype(F32)
     seen = jnp.concatenate([seen[:, :PART], seen[:, PART:]], axis=2)
     seen = seen.reshape((VIDS + 2) * PART, D).astype(BF)
@@ -334,10 +359,11 @@
     factor = 8.0 / math.sqrt(E)
     gram = nt(all_e[:COUNT], all_e[:COUNT]) * factor
 
-    frame_here = first + PART * vid + lane % PART
+    frame_here = across * COUNT + PART * vid + lane % PART
     other = jnp.zeros((COUNT, COUNT), I32)
     for m in range(VIDS):
         other = jnp.where(lane // PART == m, valid[m], other)
+    count_copy.wait_recv()
     times = count[...]
     neg = jnp.where(frame_here < other, gram, -1e30)
     top = jnp.max(jnp.where(times > 0, neg, -3e38), axis=1, keepdims=True)
@@ -347,15 +373,14 @@
 
     back_copies = [
         pltpu.make_async_remote_copy(
-            src_ref=lse_out.at[peers[k]], dst_ref=lse_in.at[vid],
-            send_sem=b_send.at[k], recv_sem=b_recv.at[k],
-            device_id={"vid": peers[k]}, device_id_type=MESH,
+            src_ref=lse_out.at[peers[k]["vid"]], dst_ref=lse_in.at[vid],
+            send_sem=b_send, recv_sem=b_recv,
+            device_id=peers[k], device_id_type=MESH,
         )
-        for k in range(1, VIDS)
+        for k in range(VIDS)
     ]
     for copy in back_copies:
         copy.start()
-    lse_in[vid] = lse_out[vid]
 
     near_e = nt(all_e[COUNT:], e)
     scores = jnp.concatenate([near_e[:REACH], near_own, near_e[REACH:]], axis=0)
@@ -367,17 +392,23 @@
     pick = iota((COUNT + 2 * REACH, COUNT), 0) == slot
     pos = jnp.sum(jnp.where(pick, scores, 0.0), axis=0, keepdims=True) * factor
 
-    for copy in back_copies:
-        copy.wait_recv()
+    pltpu.make_async_copy(lse_in, lse_in, b_recv).wait()
     back = lse_in[...].reshape(COUNT, 128)
     lse_neg = jnp.sum(jnp.where(row == lane, back, 0.0), axis=0, keepdims=True)
     peak = jnp.maximum(pos, lse_neg)
     total = peak + jnp.log(jnp.exp(pos - peak) + jnp.exp(lse_neg - peak))
     loss_out[...] = jnp.where(here < length, total - pos, 0.0)
 
-    for copy in halo_copies + pooled_copies + near_copies + back_copies:
+    for copy in halo_copies + near_copies + [count_copy]:
         copy.wait_send()
+    pltpu.make_async_copy(pack, pack, a_send).wait()
+    pltpu.make_async_copy(lse_out, lse_out, b_send).wait()
     out_copy.wait()
+
+
+def hand_over(emb, losses, emb_out, loss_out):
+    emb_out[...] = emb[...]
+    loss_out[...] = losses[...]
 
 
 def local(tokens, norm_gain, w_qkv, w_out, w_proj, offsets, negatives, valid):
@@ -405,16 +436,16 @@
             pltpu.VMEM((COUNT, VIDS * NEG), F32),
             pltpu.VMEM((2 * D, D), BF),
             pltpu.VMEM((PATCH, 160, D), BF),
-            pltpu.VMEM((PATCH, 160, D), BF),
-            pltpu.VMEM((PATCH, 4, 4, 256, 128), BF),
+            pltpu.VMEM((PATCH * 160, D), BF),
+            pltpu.VMEM((PATCH, D, COUNT), BF),
             pltpu.VMEM((4, D, 640), BF),
             pltpu.VMEM((256, D), BF),
             pltpu.VMEM((256, D), BF),
             pltpu.VMEM((4, 64, 128), F32),
-            pltpu.VMEM((4, 4, 64, 128), F32),
-            pltpu.VMEM((4, 4, 64, 128), F32),
-            pltpu.VMEM((4, 256, 128), BF),
-            pltpu.VMEM((4, 256, 128), BF),
+            pltpu.VMEM((4, 4, 64, 256), F32),
+            pltpu.VMEM((4, 4, 64, 256), F32),
+            pltpu.VMEM((4, 256, 256), BF),
+            pltpu.VMEM((4, 256, 256), BF),
             pltpu.VMEM((COUNT, D), F32),
             pltpu.VMEM((D, COUNT), F32),
             pltpu.VMEM((VIDS, 16, HALF), BF),
@@ -422,10 +453,10 @@
             pltpu.VMEM((2, 16, HALF), BF),
             pltpu.VMEM((COUNT, E), BF),
             pltpu.VMEM((COUNT, COUNT), F32),
+            pltpu.VMEM((COUNT, COUNT), F32),
             pltpu.VMEM((VIDS, PART, 128), F32),
             pltpu.VMEM((VIDS, PART, 128), F32),
-            dma((8,)), dma((7,)), dma, dma((2,)), dma((2,)), dma((VIDS,)), dma((VIDS,)),
-            dma((2,)), dma((2,)), dma((VIDS,)), dma((VIDS,)),
+            dma((8,)), dma((7,)), dma, dma((2,)), dma((2,)), dma, dma, dma((2,)), dma((2,)), dma, dma, dma, dma,
         ],
         compiler_params=pltpu.CompilerParams(
             collective_id=0, has_side_effects=True, vmem_limit_bytes=60 * 1024 * 1024
@@ -440,6 +471,15 @@
         offsets,
         jnp.swapaxes(negatives, 1, 2),
     )
+    emb, losses = pl.pallas_call(
+        hand_over,
+        out_shape=(
+            jax.ShapeDtypeStruct((COUNT, E), BF),
+            jax.ShapeDtypeStruct((1, COUNT), F32),
+        ),
+        in_specs=[vmem, vmem],
+        out_specs=(vmem, vmem),
+    )(emb, losses)
     return emb.reshape(1, COUNT, E), losses
 
 

time: 62 us -> 60.9 us (0.982)
  local copies, waits for them, and re-layouts: 2.99 us -> 0 us
  Pallas kernels: 58.2 us -> 60.1 us
    unnamed x2 -> x0, local copies, waits for them, and re-layouts: 2.99 us -> none
    pallas_call x0 -> x1, Pallas kernels: none -> 1.87 us  [local(): pl.pallas_call(hand_over, out_shape=(jax.ShapeDtypeStruct((COUNT, E), BF)...]
where the time goes in v3:
time: 60.9 us; the launch traced here: 60.8 us
  Pallas kernels  60.1 us (99%)
  between operations  0.64 us (1%)
    pallas_call x1, Pallas kernels, local(): pl.pallas_call(kernel, out_shape=(jax.ShapeDtypeStruct((COUNT, E), BF), j...  58.3 us
    pallas_call x1, Pallas kernels, local(): pl.pallas_call(hand_over, out_shape=(jax.ShapeDtypeStruct((COUNT, E), BF)...  1.87 us

profile of v3, /device:TPU:1, one launch (start us, length us, event | category | flops | bytes accessed | tf_op | source)
XLA Modules:
  0.0 60.8 jit_solution(16767109883040087124)
XLA Ops:
  0.6 58.3 %shard_map.95 = (bf16[128,2048]{1,0:T(8,128)(2,1)}, f32[1,128]{1,0:T(1,128)}) custom-call(s32[16]{0:T(128)} %valid.1, bf16[2048,1024]{1,0:T(8,128)(2,1)} %bitcast.4, f32[1,1024]{1,0:T(1,128)} %bitcast.6, bf16[1024,3072]{1,0:T(8,128)(2,1)} %w_qkv.1, bf16[1024,1024]{1,0:T(8,128)(2,1)} %w_out.1, bf16[1024,2048]{1,0:T(8,128)(2,1)} %w_proj.1, s32[1,128]{1,0:T(1,128)} %offsets.1, ...), custom_call_target="tpu_custom_call" | custom-call | tf_op jit(solution)/shard_map/pallas_call | solution.py:418
  58.9 1.9 %shard_map.96 = (bf16[128,2048]{1,0:T(8,128)(2,1)}, f32[1,128]{1,0:T(1,128)}) custom-call(bf16[128,2048]{1,0:T(8,128)(2,1)} %get-tuple-element.6.emb, f32[1,128]{1,0:T(1,128)} %get-tuple-element.7.losses), custom_call_target="tpu_custom_call" | custom-call | tf_op jit(solution)/shard_map/pallas_call | solution.py:474

commit v4 on v3

--- a/solution.py
+++ b/solution.py
@@ -38,7 +38,7 @@
 def kernel(
     valid, tokens, gain, w_qkv, w_out, w_proj, offsets, negatives,
     emb_out, loss_out,
-    raw, halo, wq, wk, wv, wo, negs, negt, wqvt, xn, keys, qt, vt, y0, y1,
+    perm, eye, avg, raw, halo, wq, wk, wv, wo, wp, negs, negt, wvt, xn, keys, queries, vt, y0, y1,
     bias, st0, st1, pr0, pr1, tokmean, acc, pack, got, near, own_e, count_out, count, lse_out, lse_in,
     tok_sem, w_sem, out_sem, halo_send, halo_recv, a_send, a_recv, n_send, n_recv, b_send, b_recv, c_send, c_recv,
 ):
@@ -47,7 +47,11 @@
     left = lax.rem(tm + TMS - 1, TMS)
     right = lax.rem(tm + 1, TMS)
     across = lax.rem(tm + TMS // 2, TMS)
-    peers = [{"vid": lax.rem(vid + k, VIDS), "tm": across} for k in range(VIDS)]
+    y_hi, z, core = vid // 8, vid // 2 % 4, vid % 2
+    peers = [
+        {"vid": (y_hi + dy) % 2 * 8 + (z + dz) % 4 * 2 + (core + dc) % 2, "tm": across}
+        for dz in (2, 1, 3, 0) for dy in (1, 0) for dc in (1, 0)
+    ]
     first = tm * COUNT
     length = valid[vid]
 
@@ -59,32 +63,37 @@
         pltpu.make_async_copy(src, dst, w_sem.at[i])
         for i, (src, dst) in enumerate(
             [
+                (w_qkv.at[:, pl.ds(2 * D, D)], wv),
+                (negatives, negs),
                 (w_qkv.at[:, pl.ds(0, D)], wq),
-                (w_qkv.at[:, pl.ds(2 * D, D)], wv),
                 (w_qkv.at[:, pl.ds(D, D)], wk),
-                (w_out, wo),
-                (negatives, negs),
-                (w_proj.at[:, pl.ds(0, D)], wq),
-                (w_proj.at[:, pl.ds(D, D)], wv),
+                (w_proj, wp),
             ]
         )
+    ]
+    out_copies = [
+        pltpu.make_async_copy(
+            w_out.at[pl.ds(256 * (2 * jp + j2) + 64 * h, 64)],
+            wo.at[pl.ds(512 * jp + 128 * h + 64 * j2, 64)],
+            w_sem.at[5],
+        )
+        for jp in range(2) for h in range(4) for j2 in range(2)
     ]
     barrier = pltpu.get_barrier_semaphore()
     for peer in peers:
         pl.semaphore_signal(barrier, inc=1, device_id=peer, device_id_type=MESH)
     for peer in (left, right):
         pl.semaphore_signal(barrier, inc=1, device_id={"tm": peer}, device_id_type=MESH)
+    w_copies[1].start()
+    tok_copies[0].start()
     w_copies[0].start()
-    tok_copies[0].start()
-    w_copies[1].start()
-    for copy in tok_copies[1:]:
+    for copy in tok_copies[1:] + w_copies[2:] + out_copies:
         copy.start()
-    for copy in w_copies[2:5]:
-        copy.start()
+
     r0, r1 = iota((256, 256), 0), iota((256, 256), 1)
-    perm = (r1 == (r0 % 16) * 16 + r0 // 16).astype(F32).astype(BF)
-    eye = (r0 == r1).astype(F32).astype(BF)
-    avg = jnp.where(iota((16, 256), 0) == iota((16, 256), 1) // 16, 1.0 / PATCH, 0.0).astype(BF)
+    perm[...] = (r1 == (r0 % 16) * 16 + r0 // 16).astype(F32).astype(BF)
+    eye[...] = (r0 == r1).astype(F32).astype(BF)
+    avg[...] = jnp.where(iota((16, 256), 0) == iota((16, 256), 1) // 16, 1.0 / PATCH, 0.0).astype(BF)
 
     g0, f0 = iota((64, 128), 0), iota((64, 128), 1) % 32
     for b in range(4):
@@ -96,7 +105,7 @@
         bias[b] = jnp.where(ok, 0.0, -1e30)
     lane_block = iota((64, 128), 1) // 32
 
-    w_copies[4].wait()
+    w_copies[1].wait()
     lane = iota((COUNT, COUNT), 1)
     row = iota((COUNT, COUNT), 0)
     negt[...] = jnp.transpose(negs[...].reshape(VIDS * NEG, COUNT).astype(F32))
@@ -108,23 +117,6 @@
         times += (one * PART + (row % PART).astype(F32) == lane.astype(F32)).astype(F32)
     count_out[...] = times
 
-    w_copies[0].wait()
-
-    def flip(src, base):
-        def body(i, carry):
-            a = pl.multiple_of(i * 256, 256)
-            for c in range(4):
-                block = nt(eye, src[256 * c:256 * c + 256, pl.ds(a, 256)])
-                wqvt[pl.ds(base + a, 256), 256 * c:256 * c + 256] = block.astype(BF)
-            return carry
-        lax.fori_loop(0, 4, body, 0)
-
-    flip(wq, 0)
-    w_copies[1].wait()
-    flip(wv, D)
-    w_copies[5].start()
-    w_copies[6].start()
-
     pl.semaphore_wait(barrier, VIDS + 2)
 
     halo_copies = [
@@ -143,7 +135,7 @@
         copy.start()
 
     count_copy = pltpu.make_async_remote_copy(
-        src_ref=count_out, dst_ref=count, send_sem=c_send, recv_sem=c_recv, device_id=peers[0], device_id_type=MESH,
+        src_ref=count_out, dst_ref=count, send_sem=c_send, recv_sem=c_recv, device_id=peers[-1], device_id_type=MESH,
     )
     count_copy.start()
 
@@ -158,78 +150,83 @@
 
     def permuted(y, rows):
         for c in range(4):
-            part = nn(perm, y[:, 256 * c:256 * c + 256]).astype(BF)
+            part = nn(perm[...], y[:, 256 * c:256 * c + 256]).astype(BF)
             xn[:, rows, 256 * c:256 * c + 256] = part.reshape(PATCH, 16, 256)
             yield
 
     def averaged(b):
-        tokmean[pl.ds(pl.multiple_of(16 * b, 16), 16), :] = nn(avg, raw[b])
+        tokmean[pl.ds(pl.multiple_of(16 * b, 16), 16), :] = nn(avg[...], raw[b])
         yield
 
     def rows_of(b):
         return pl.ds(pl.multiple_of(16 * b + 16, 16), 16)
+
+    def flip(a):
+        for c in range(4):
+            block = nt(eye[...], wv[256 * c:256 * c + 256, pl.ds(a, 256)])
+            wvt[pl.ds(a, 256), 256 * c:256 * c + 256] = block.astype(BF)
+            yield
 
     def weave(*jobs):
         for _ in itertools.zip_longest(*jobs):
             pass
 
-    for b in range(8):
-        tok_copies[b].wait()
+    def arrived(b):
+        pltpu.make_async_copy(tokens.at[pl.ds(0, 256)], raw.at[b], tok_sem.at[b]).wait()
+
+    arrived(0)
     weave(normed(raw.at[0], y0))
+    w_copies[0].wait()
 
     def norm_pair(i, carry):
         b = 2 * i
-        weave(permuted(y0, rows_of(b)), normed(raw.at[b + 1], y1), averaged(b))
+        arrived(b + 1)
+        arrived(b + 2)
+        weave(permuted(y0, rows_of(b)), normed(raw.at[b + 1], y1), averaged(b), flip(pl.multiple_of(256 * i, 256)))
         weave(permuted(y1, rows_of(b + 1)), normed(raw.at[b + 2], y0), averaged(b + 1))
         return carry
 
     lax.fori_loop(0, 3, norm_pair, 0)
-    weave(permuted(y0, rows_of(6)), normed(raw.at[7], y1), averaged(6))
+    arrived(7)
+    weave(permuted(y0, rows_of(6)), normed(raw.at[7], y1), averaged(6), flip(768))
     weave(permuted(y1, rows_of(7)), averaged(7))
 
+    w_copies[2].wait()
     scale = math.log2(math.e) / 8.0
 
-    def queries(i, carry):
-        x2 = xn[pl.ds(2 * i, 2), 16:16 + COUNT, :].reshape(256, D)
+    def project_queries(i, carry):
+        rows = pl.ds(pl.multiple_of(512 * i, 512), 512)
+        x = xn[pl.ds(4 * i, 4), 16:16 + COUNT, :].reshape(512, D)
         for c in range(2):
-            r = nt(wqvt[512 * c:512 * c + 512], x2) * scale
-            for u in range(2):
-                for n in range(8):
-                    part = r[64 * n:64 * n + 64, COUNT * u:COUNT * u + COUNT]
-                    if n % 4:
-                        part = pltpu.roll(part, 32 * (n % 4), 1)
-                    qt[2 * i + u, 512 * c + 64 * n:512 * c + 64 * n + 64, :] = part.astype(BF)
+            queries[rows, 512 * c:512 * c + 512] = (nn(x, wq[:, 512 * c:512 * c + 512]) * scale).astype(BF)
         return carry
 
-    lax.fori_loop(0, 8, queries, 0)
+    lax.fori_loop(0, 4, project_queries, 0)
 
     def values(ga, ra, gb, rb):
         xa = xn[pl.ds(4 * ga, 4), 32 * ra:32 * ra + 32, :].reshape(128, D)
         xb = xn[pl.ds(4 * gb, 4), 32 * rb:32 * rb + 32, :].reshape(128, D)
         x2 = jnp.concatenate([xa, xb], axis=0)
         for c in range(2):
-            r = nt(wqvt[D + 512 * c:D + 512 * c + 512], x2).astype(BF)
+            r = nt(wvt[512 * c:512 * c + 512], x2).astype(BF)
             vt[ga, 512 * c:512 * c + 512, 128 * ra:128 * ra + 128] = r[:, :128]
             vt[gb, 512 * c:512 * c + 512, 128 * rb:128 * rb + 128] = r[:, 128:]
-
-    def values_inner(g, carry):
-        values(g, 1, g, 2)
+            yield
+
+    def values_inner(i, carry):
+        weave(values(2 * i, 1, 2 * i, 2))
+        weave(values(2 * i + 1, 1, 2 * i + 1, 2))
         return carry
 
-    def values_last(g, carry):
-        values(2 * g, 3, 2 * g + 1, 3)
-        return carry
-
-    lax.fori_loop(0, 4, values_inner, 0)
-    lax.fori_loop(0, 2, values_last, 0)
+    lax.fori_loop(0, 2, values_inner, 0)
 
     halo_copies[0].wait_recv()
     halo_copies[1].wait_recv()
-    weave(normed(halo.at[0], y0))
-    weave(permuted(y0, pl.ds(0, 16)), normed(halo.at[1], y1))
-    weave(permuted(y1, pl.ds(16 + COUNT, 16)))
-
-    w_copies[2].wait()
+    weave(values(0, 3, 1, 3), normed(halo.at[0], y0))
+    weave(values(2, 3, 3, 3), normed(halo.at[1], y1))
+    weave(permuted(y0, pl.ds(0, 16)), permuted(y1, pl.ds(16 + COUNT, 16)))
+
+    w_copies[3].wait()
 
     def project_keys(i, carry):
         rows = pl.ds(pl.multiple_of(512 * i, 512), 512)
@@ -239,30 +236,33 @@
 
     lax.fori_loop(0, 5, project_keys, 0)
 
-    def values_outer(g, carry):
-        values(g, 0, g, 4)
+    def values_outer(i, carry):
+        weave(values(2 * i, 0, 2 * i, 4))
+        weave(values(2 * i + 1, 0, 2 * i + 1, 4))
         return carry
 
-    lax.fori_loop(0, 4, values_outer, 0)
+    lax.fori_loop(0, 2, values_outer, 0)
 
     acc[...] = jnp.zeros_like(acc)
 
     def where_is(u):
         return u // 2, pl.ds(pl.multiple_of(512 * (u % 2), 512), 512)
 
-    diagonal = [jnp.concatenate([lane_block == (b + h) % 4 for h in range(4)] * 2, axis=0) for b in range(4)]
+    head_lanes = [iota((32, 256), 1) // 64 == h for h in range(4)]
+
+    def diagonal(x):
+        return [jnp.where(head_lanes[h], x, jnp.zeros_like(x)) for h in range(4)]
 
     def scores_of(u, out):
         g, cols = where_is(u)
         for q in range(4):
             p = 4 * g + q
             for b in range(4):
-                q8 = qt[p, cols, :]
-                q8 = jnp.where(diagonal[b], q8, jnp.zeros_like(q8))
+                q8 = queries[pl.ds(pl.multiple_of(COUNT * p + 32 * b, 32), 32), cols]
                 k8 = keys[pl.ds(pl.multiple_of(160 * p + 32 * b, 32), 64), cols]
-                r = nn(
+                r = nt(
                     jnp.concatenate([k8[:, :256], k8[:, 256:]], axis=0),
-                    jnp.concatenate([q8[:256], q8[256:]], axis=1),
+                    jnp.concatenate(diagonal(q8[:, :256]) + diagonal(q8[:, 256:]), axis=0),
                 )
                 out[q, b, :, :128] = r[:64, :128]
                 out[q, b, :, 128:] = r[64:, 128:]
@@ -282,14 +282,13 @@
     def attended_of(u, probs):
         g, rows = where_is(u)
         for b in range(4):
-            r = nn(vt[g, rows, 128 * b:128 * b + 256], probs[b])
             for j in range(2):
-                for h in range(4):
-                    at = 256 * j + 64 * h
-                    part = r[at:at + 64, 128 * j:128 * j + 128]
-                    where = pl.ds(pl.multiple_of(512 * (u % 2) + at, 64), 64)
-                    acc[where, :] += jnp.where(lane_block == (b + h) % 4, part, 0.0)
-            for _ in range(4):
+                r = nn(vt[g, pl.ds(pl.multiple_of(512 * (u % 2) + 256 * j, 256), 256), 128 * b:128 * b + 256], probs[b, :, 128 * j:128 * j + 128])
+                part = r[:64]
+                for h in range(1, 4):
+                    part = jnp.where(lane_block == h, r[64 * h:64 * h + 64], part)
+                acc[u % 2, b, 64 * j:64 * j + 64, :] += part
+                yield
                 yield
 
     weave(scores_of(0, st0))
@@ -305,13 +304,12 @@
     weave(softmax_of(st1, pr1), attended_of(6, pr0))
     weave(attended_of(7, pr1))
 
-    w_copies[3].wait()
-    heads = []
-    for h in range(16):
-        part = acc[64 * h:64 * h + 64, :]
-        heads.append(pltpu.roll(part, 128 - 32 * (h % 4), 1) if h % 4 else part)
-    att = jnp.transpose(jnp.concatenate(heads, axis=0) * (1.0 / PATCH)).astype(BF)
-    pooled = tokmean[...] + nn(att, wo[...])
+    pltpu.make_async_copy(w_out, wo, w_sem.at[5]).wait()
+    att = []
+    for b in range(4):
+        turned = [jnp.transpose(acc[jp, b] * (1.0 / PATCH)).astype(BF) for jp in range(2)]
+        att.append(jnp.concatenate([t[32 * h:32 * h + 32] for t in turned for h in range(4)], axis=1))
+    pooled = tokmean[...] + nn(jnp.concatenate(att, axis=0), wo[...])
     blocks = pooled.reshape(VIDS, PART, D)
     pack[...] = jnp.concatenate([blocks[:, :, :HALF], blocks[:, :, HALF:]], axis=1).astype(BF)
 
@@ -338,11 +336,8 @@
     for copy in pooled_copies + near_copies:
         copy.start()
 
-    w_copies[5].wait()
-    w_copies[6].wait()
-    mine = pooled.astype(BF)
-    own_e[:, :D] = nn(mine, wq[...]).astype(BF)
-    own_e[:, D:] = nn(mine, wv[...]).astype(BF)
+    w_copies[4].wait()
+    own_e[...] = nn(pooled.astype(BF), wp[...]).astype(BF)
     out_copy = pltpu.make_async_copy(own_e, emb_out, out_sem)
     out_copy.start()
 
@@ -355,7 +350,7 @@
     seen = jnp.concatenate([got[...], near[...]], axis=0).astype(F32)
     seen = jnp.concatenate([seen[:, :PART], seen[:, PART:]], axis=2)
     seen = seen.reshape((VIDS + 2) * PART, D).astype(BF)
-    all_e = jnp.concatenate([nn(seen, wq[...]).astype(BF), nn(seen, wv[...]).astype(BF)], axis=1)
+    all_e = nn(seen, wp[...]).astype(BF)
     factor = 8.0 / math.sqrt(E)
     gram = nt(all_e[:COUNT], all_e[:COUNT]) * factor
 
@@ -426,18 +421,22 @@
         ],
         out_specs=(anywhere, vmem),
         scratch_shapes=[
+            pltpu.VMEM((256, 256), BF),
+            pltpu.VMEM((256, 256), BF),
+            pltpu.VMEM((16, 256), BF),
             pltpu.VMEM((8, 256, D), BF),
             pltpu.VMEM((2, 256, D), BF),
             pltpu.VMEM((D, D), BF),
             pltpu.VMEM((D, D), BF),
             pltpu.VMEM((D, D), BF),
             pltpu.VMEM((D, D), BF),
+            pltpu.VMEM((D, E), BF),
             pltpu.VMEM((VIDS, NEG, COUNT), I32),
             pltpu.VMEM((COUNT, VIDS * NEG), F32),
-            pltpu.VMEM((2 * D, D), BF),
+            pltpu.VMEM((D, D), BF),
             pltpu.VMEM((PATCH, 160, D), BF),
             pltpu.VMEM((PATCH * 160, D), BF),
-            pltpu.VMEM((PATCH, D, COUNT), BF),
+            pltpu.VMEM((PATCH * COUNT, D), BF),
             pltpu.VMEM((4, D, 640), BF),
             pltpu.VMEM((256, D), BF),
             pltpu.VMEM((256, D), BF),
@@ -447,7 +446,7 @@
             pltpu.VMEM((4, 256, 256), BF),
             pltpu.VMEM((4, 256, 256), BF),
             pltpu.VMEM((COUNT, D), F32),
-            pltpu.VMEM((D, COUNT), F32),
+            pltpu.VMEM((2, 4, 128, 128), F32),
             pltpu.VMEM((VIDS, 16, HALF), BF),
             pltpu.VMEM((VIDS, 16, HALF), BF),
             pltpu.VMEM((2, 16, HALF), BF),
@@ -456,7 +455,7 @@
             pltpu.VMEM((COUNT, COUNT), F32),
             pltpu.VMEM((VIDS, PART, 128), F32),
             pltpu.VMEM((VIDS, PART, 128), F32),
-            dma((8,)), dma((7,)), dma, dma((2,)), dma((2,)), dma, dma, dma((2,)), dma((2,)), dma, dma, dma, dma,
+            dma((8,)), dma((6,)), dma, dma((2,)), dma((2,)), dma, dma, dma((2,)), dma((2,)), dma, dma, dma, dma,
         ],
         compiler_params=pltpu.CompilerParams(
             collective_id=0, has_side_effects=True, vmem_limit_bytes=60 * 1024 * 1024

time: 60.9 us -> 56.9 us (0.934)
  Pallas kernels: 60.1 us -> 56.1 us
    pallas_call x1, Pallas kernels: 58.3 us -> 54.3 us  [local(): pl.pallas_call(kernel, out_shape=(jax.ShapeDtypeStruct((COUNT, E), BF), j...]
where the time goes in v4:
time: 56.9 us; the launch traced here: 56.8 us
  Pallas kernels  56.1 us (99%)
  between operations  0.64 us (1%)
    pallas_call x1, Pallas kernels, local(): pl.pallas_call(kernel, out_shape=(jax.ShapeDtypeStruct((COUNT, E), BF), j...  54.3 us
    pallas_call x1, Pallas kernels, local(): pl.pallas_call(hand_over, out_shape=(jax.ShapeDtypeStruct((COUNT, E), BF)...  1.87 us

profile of v4, /device:TPU:1, one launch (start us, length us, event | category | flops | bytes accessed | tf_op | source)
XLA Modules:
  0.0 56.8 jit_solution(14795576262579012120)
XLA Ops:
  0.6 54.3 %shard_map.95 = (bf16[128,2048]{1,0:T(8,128)(2,1)}, f32[1,128]{1,0:T(1,128)}) custom-call(s32[16]{0:T(128)} %valid.1, bf16[2048,1024]{1,0:T(8,128)(2,1)} %bitcast.4, f32[1,1024]{1,0:T(1,128)} %bitcast.6, bf16[1024,3072]{1,0:T(8,128)(2,1)} %w_qkv.1, bf16[1024,1024]{1,0:T(8,128)(2,1)} %w_out.1, bf16[1024,2048]{1,0:T(8,128)(2,1)} %w_proj.1, s32[1,128]{1,0:T(1,128)} %offsets.1, ...), custom_call_target="tpu_custom_call" | custom-call | tf_op jit(solution)/shard_map/pallas_call | solution.py:413
  54.9 1.9 %shard_map.96 = (bf16[128,2048]{1,0:T(8,128)(2,1)}, f32[1,128]{1,0:T(1,128)}) custom-call(bf16[128,2048]{1,0:T(8,128)(2,1)} %get-tuple-element.6.emb, f32[1,128]{1,0:T(1,128)} %get-tuple-element.7.losses), custom_call_target="tpu_custom_call" | custom-call | tf_op jit(solution)/shard_map/pallas_call | solution.py:473

commit v5 on v4

--- a/solution.py
+++ b/solution.py
@@ -87,7 +87,7 @@
     w_copies[1].start()
     tok_copies[0].start()
     w_copies[0].start()
-    for copy in tok_copies[1:] + w_copies[2:] + out_copies:
+    for copy in tok_copies[1:]:
         copy.start()
 
     r0, r1 = iota((256, 256), 0), iota((256, 256), 1)
@@ -177,6 +177,7 @@
     arrived(0)
     weave(normed(raw.at[0], y0))
     w_copies[0].wait()
+    w_copies[2].start()
 
     def norm_pair(i, carry):
         b = 2 * i
@@ -190,6 +191,7 @@
     arrived(7)
     weave(permuted(y0, rows_of(6)), normed(raw.at[7], y1), averaged(6), flip(768))
     weave(permuted(y1, rows_of(7)), averaged(7))
+    w_copies[3].start()
 
     w_copies[2].wait()
     scale = math.log2(math.e) / 8.0
@@ -202,6 +204,9 @@
         return carry
 
     lax.fori_loop(0, 4, project_queries, 0)
+
+    for copy in w_copies[4:] + out_copies:
+        copy.start()
 
     def values(ga, ra, gb, rb):
         xa = xn[pl.ds(4 * ga, 4), 32 * ra:32 * ra + 32, :].reshape(128, D)
@@ -246,68 +251,60 @@
     acc[...] = jnp.zeros_like(acc)
 
     def where_is(u):
-        return u // 2, pl.ds(pl.multiple_of(512 * (u % 2), 512), 512)
+        return u // 4, pl.ds(pl.multiple_of(256 * (u % 4), 256), 256)
 
     head_lanes = [iota((32, 256), 1) // 64 == h for h in range(4)]
 
     def diagonal(x):
         return [jnp.where(head_lanes[h], x, jnp.zeros_like(x)) for h in range(4)]
 
-    def scores_of(u, out):
+    def probs_of(u, out):
         g, cols = where_is(u)
         for q in range(4):
-            p = 4 * g + q
             for b in range(4):
-                q8 = queries[pl.ds(pl.multiple_of(COUNT * p + 32 * b, 32), 32), cols]
-                k8 = keys[pl.ds(pl.multiple_of(160 * p + 32 * b, 32), 64), cols]
-                r = nt(
-                    jnp.concatenate([k8[:, :256], k8[:, 256:]], axis=0),
-                    jnp.concatenate(diagonal(q8[:, :256]) + diagonal(q8[:, 256:]), axis=0),
-                )
-                out[q, b, :, :128] = r[:64, :128]
-                out[q, b, :, 128:] = r[64:, 128:]
-                yield
-
-    def softmax_of(src, out):
-        for q in range(4):
-            for b in range(4):
-                for j in range(2):
-                    s = src[q, b, :, 128 * j:128 * j + 128] + bias[b]
+                ps = [8 * g + 2 * q, 8 * g + 2 * q + 1]
+                q2 = [queries[pl.ds(pl.multiple_of(COUNT * p + 32 * b, 32), 32), cols] for p in ps]
+                k2 = [keys[pl.ds(pl.multiple_of(160 * p + 32 * b, 32), 64), cols] for p in ps]
+                r = nt(jnp.concatenate(k2, axis=0), jnp.concatenate(diagonal(q2[0]) + diagonal(q2[1]), axis=0))
+                for n in range(2):
+                    s = r[64 * n:64 * n + 64, 128 * n:128 * n + 128] + bias[b]
                     e = jnp.exp2(s - jnp.max(s, axis=0, keepdims=True))
                     e = (e * (1.0 / jnp.sum(e, axis=0, keepdims=True))).astype(BF)
-                    out[b, 32 * q:32 * q + 32, 128 * j:128 * j + 128] = e[:32]
-                    out[b, 128 + 32 * q:128 + 32 * q + 32, 128 * j:128 * j + 128] = e[32:]
+                    at = 256 * (q // 2) + 64 * (q % 2) + 32 * n
+                    out[b, at:at + 32, :] = e[:32]
+                    out[b, 128 + at:128 + at + 32, :] = e[32:]
                 yield
 
     def attended_of(u, probs):
         g, rows = where_is(u)
         for b in range(4):
-            for j in range(2):
-                r = nn(vt[g, pl.ds(pl.multiple_of(512 * (u % 2) + 256 * j, 256), 256), 128 * b:128 * b + 256], probs[b, :, 128 * j:128 * j + 128])
-                part = r[:64]
-                for h in range(1, 4):
-                    part = jnp.where(lane_block == h, r[64 * h:64 * h + 64], part)
-                acc[u % 2, b, 64 * j:64 * j + 64, :] += part
+            lanes = slice(128 * b, 128 * b + 256)
+            v = jnp.concatenate([vt[2 * g, rows, lanes], vt[2 * g + 1, rows, lanes]], axis=1)
+            r = nn(v, probs[b])
+            part = r[:64]
+            for h in range(1, 4):
+                part = jnp.where(lane_block == h, r[64 * h:64 * h + 64], part)
+            acc[u % 4, b] += part
+            for _ in range(4):
                 yield
-                yield
-
-    weave(scores_of(0, st0))
-    weave(scores_of(1, st1), softmax_of(st0, pr0))
+
+    weave(probs_of(0, pr0))
 
     def attend(i, carry):
         u = 2 * i
-        weave(scores_of(u + 2, st0), softmax_of(st1, pr1), attended_of(u, pr0))
-        weave(scores_of(u + 3, st1), softmax_of(st0, pr0), attended_of(u + 1, pr1))
+        weave(probs_of(u + 1, pr1), attended_of(u, pr0))
+        weave(probs_of(u + 2, pr0), attended_of(u + 1, pr1))
         return carry
 
     lax.fori_loop(0, 3, attend, 0)
-    weave(softmax_of(st1, pr1), attended_of(6, pr0))
+    weave(probs_of(7, pr1), attended_of(6, pr0))
     weave(attended_of(7, pr1))
 
     pltpu.make_async_copy(w_out, wo, w_sem.at[5]).wait()
     att = []
     for b in range(4):
-        turned = [jnp.transpose(acc[jp, b] * (1.0 / PATCH)).astype(BF) for jp in range(2)]
+        pairs = [jnp.concatenate([acc[2 * jp, b], acc[2 * jp + 1, b]], axis=0) for jp in range(2)]
+        turned = [jnp.transpose(pair * (1.0 / PATCH)).astype(BF) for pair in pairs]
         att.append(jnp.concatenate([t[32 * h:32 * h + 32] for t in turned for h in range(4)], axis=1))
     pooled = tokmean[...] + nn(jnp.concatenate(att, axis=0), wo[...])
     blocks = pooled.reshape(VIDS, PART, D)
@@ -443,10 +440,10 @@
             pltpu.VMEM((4, 64, 128), F32),
             pltpu.VMEM((4, 4, 64, 256), F32),
             pltpu.VMEM((4, 4, 64, 256), F32),
-            pltpu.VMEM((4, 256, 256), BF),
-            pltpu.VMEM((4, 256, 256), BF),
+            pltpu.VMEM((4, 512, 128), BF),
+            pltpu.VMEM((4, 512, 128), BF),
             pltpu.VMEM((COUNT, D), F32),
-            pltpu.VMEM((2, 4, 128, 128), F32),
+            pltpu.VMEM((4, 4, 64, 128), F32),
             pltpu.VMEM((VIDS, 16, HALF), BF),
             pltpu.VMEM((VIDS, 16, HALF), BF),
             pltpu.VMEM((2, 16, HALF), BF),

time: 56.9 us -> 56.9 us (level)
  no operation moved by 1% of the time
where the time goes in v5:
time: 56.9 us; the launch traced here: 56.7 us
  Pallas kernels  56.1 us (99%)
  between operations  0.64 us (1%)
    pallas_call x1, Pallas kernels, local(): pl.pallas_call(kernel, out_shape=(jax.ShapeDtypeStruct((COUNT, E), BF), j...  54.2 us
    pallas_call x1, Pallas kernels, local(): pl.pallas_call(hand_over, out_shape=(jax.ShapeDtypeStruct((COUNT, E), BF)...  1.87 us

profile of v5, /device:TPU:1, one launch (start us, length us, event | category | flops | bytes accessed | tf_op | source)
XLA Modules:
  0.0 56.7 jit_solution(15584986084091805300)
XLA Ops:
  0.6 54.2 %shard_map.95 = (bf16[128,2048]{1,0:T(8,128)(2,1)}, f32[1,128]{1,0:T(1,128)}) custom-call(s32[16]{0:T(128)} %valid.1, bf16[2048,1024]{1,0:T(8,128)(2,1)} %bitcast.4, f32[1,1024]{1,0:T(1,128)} %bitcast.6, bf16[1024,3072]{1,0:T(8,128)(2,1)} %w_qkv.1, bf16[1024,1024]{1,0:T(8,128)(2,1)} %w_out.1, bf16[1024,2048]{1,0:T(8,128)(2,1)} %w_proj.1, s32[1,128]{1,0:T(1,128)} %offsets.1, ...), custom_call_target="tpu_custom_call" | custom-call | tf_op jit(solution)/shard_map/pallas_call | solution.py:410
  54.8 1.9 %shard_map.96 = (bf16[128,2048]{1,0:T(8,128)(2,1)}, f32[1,128]{1,0:T(1,128)}) custom-call(bf16[128,2048]{1,0:T(8,128)(2,1)} %get-tuple-element.6.emb, f32[1,128]{1,0:T(1,128)} %get-tuple-element.7.losses), custom_call_target="tpu_custom_call" | custom-call | tf_op jit(solution)/shard_map/pallas_call | solution.py:470

commit v6 on v5

--- a/solution.py
+++ b/solution.py
@@ -225,21 +225,33 @@
 
     lax.fori_loop(0, 2, values_inner, 0)
 
+    weave(values(0, 3, 1, 3))
+    weave(values(2, 3, 3, 3))
+
+    w_copies[3].wait()
+
+    def own_keys(i):
+        x = xn[pl.ds(4 * i, 4), 16:16 + COUNT, :].reshape(512, D)
+        for c in range(2):
+            r = nn(x, wk[:, 512 * c:512 * c + 512]).astype(BF)
+            keys[pl.ds(4 * i, 4), 16:16 + COUNT, 512 * c:512 * c + 512] = r.reshape(4, COUNT, 512)
+            yield
+
+    def project_keys(i, carry):
+        weave(own_keys(i))
+        return carry
+
+    lax.fori_loop(0, 3, project_keys, 0)
+
     halo_copies[0].wait_recv()
     halo_copies[1].wait_recv()
-    weave(values(0, 3, 1, 3), normed(halo.at[0], y0))
-    weave(values(2, 3, 3, 3), normed(halo.at[1], y1))
+    weave(own_keys(3), normed(halo.at[0], y0), normed(halo.at[1], y1))
     weave(permuted(y0, pl.ds(0, 16)), permuted(y1, pl.ds(16 + COUNT, 16)))
-
-    w_copies[3].wait()
-
-    def project_keys(i, carry):
-        rows = pl.ds(pl.multiple_of(512 * i, 512), 512)
-        for c in range(2):
-            keys[rows, 512 * c:512 * c + 512] = nn(xn.reshape(PATCH * 160, D)[rows, :], wk[:, 512 * c:512 * c + 512]).astype(BF)
-        return carry
-
-    lax.fori_loop(0, 5, project_keys, 0)
+    x = jnp.concatenate([xn[:, :16, :], xn[:, 16 + COUNT:, :]], axis=1).reshape(512, D)
+    for c in range(2):
+        r = nn(x, wk[:, 512 * c:512 * c + 512]).astype(BF).reshape(PATCH, 32, 512)
+        keys[:, :16, 512 * c:512 * c + 512] = r[:, :16]
+        keys[:, 16 + COUNT:, 512 * c:512 * c + 512] = r[:, 16:]
 
     def values_outer(i, carry):
         weave(values(2 * i, 0, 2 * i, 4))
@@ -264,7 +276,7 @@
             for b in range(4):
                 ps = [8 * g + 2 * q, 8 * g + 2 * q + 1]
                 q2 = [queries[pl.ds(pl.multiple_of(COUNT * p + 32 * b, 32), 32), cols] for p in ps]
-                k2 = [keys[pl.ds(pl.multiple_of(160 * p + 32 * b, 32), 64), cols] for p in ps]
+                k2 = [keys[p, 32 * b:32 * b + 64, cols] for p in ps]
                 r = nt(jnp.concatenate(k2, axis=0), jnp.concatenate(diagonal(q2[0]) + diagonal(q2[1]), axis=0))
                 for n in range(2):
                     s = r[64 * n:64 * n + 64, 128 * n:128 * n + 128] + bias[b]
@@ -432,7 +444,7 @@
             pltpu.VMEM((COUNT, VIDS * NEG), F32),
             pltpu.VMEM((D, D), BF),
             pltpu.VMEM((PATCH, 160, D), BF),
-            pltpu.VMEM((PATCH * 160, D), BF),
+            pltpu.VMEM((PATCH, 160, D), BF),
             pltpu.VMEM((PATCH * COUNT, D), BF),
             pltpu.VMEM((4, D, 640), BF),
             pltpu.VMEM((256, D), BF),

time: 56.9 us -> 53.3 us (0.937)
  Pallas kernels: 56.1 us -> 52.5 us
    pallas_call x1, Pallas kernels: 54.2 us -> 50.7 us  [local(): pl.pallas_call(kernel, out_shape=(jax.ShapeDtypeStruct((COUNT, E), BF), j...]
where the time goes in v6:
time: 53.3 us; the launch traced here: 53.2 us
  Pallas kernels  52.5 us (98%)
  between operations  0.64 us (1%)
    pallas_call x1, Pallas kernels, local(): pl.pallas_call(kernel, out_shape=(jax.ShapeDtypeStruct((COUNT, E), BF), j...  50.7 us
    pallas_call x1, Pallas kernels, local(): pl.pallas_call(hand_over, out_shape=(jax.ShapeDtypeStruct((COUNT, E), BF)...  1.87 us

profile of v6, /device:TPU:1, one launch (start us, length us, event | category | flops | bytes accessed | tf_op | source)
XLA Modules:
  0.0 53.2 jit_solution(5612481718949713031)
XLA Ops:
  0.6 50.7 %shard_map.95 = (bf16[128,2048]{1,0:T(8,128)(2,1)}, f32[1,128]{1,0:T(1,128)}) custom-call(s32[16]{0:T(128)} %valid.1, bf16[2048,1024]{1,0:T(8,128)(2,1)} %bitcast.4, f32[1,1024]{1,0:T(1,128)} %bitcast.6, bf16[1024,3072]{1,0:T(8,128)(2,1)} %w_qkv.1, bf16[1024,1024]{1,0:T(8,128)(2,1)} %w_out.1, bf16[1024,2048]{1,0:T(8,128)(2,1)} %w_proj.1, s32[1,128]{1,0:T(1,128)} %offsets.1, ...), custom_call_target="tpu_custom_call" | custom-call | tf_op jit(solution)/shard_map/pallas_call | solution.py:422
  51.3 1.9 %shard_map.96 = (bf16[128,2048]{1,0:T(8,128)(2,1)}, f32[1,128]{1,0:T(1,128)}) custom-call(bf16[128,2048]{1,0:T(8,128)(2,1)} %get-tuple-element.6.emb, f32[1,128]{1,0:T(1,128)} %get-tuple-element.7.losses), custom_call_target="tpu_custom_call" | custom-call | tf_op jit(solution)/shard_map/pallas_call | solution.py:482

commit v7 on v6

--- a/solution.py
+++ b/solution.py
@@ -86,7 +86,6 @@
         pl.semaphore_signal(barrier, inc=1, device_id={"tm": peer}, device_id_type=MESH)
     w_copies[1].start()
     tok_copies[0].start()
-    w_copies[0].start()
     for copy in tok_copies[1:]:
         copy.start()
 
@@ -163,8 +162,7 @@
 
     def flip(a):
         for c in range(4):
-            block = nt(eye[...], wv[256 * c:256 * c + 256, pl.ds(a, 256)])
-            wvt[pl.ds(a, 256), 256 * c:256 * c + 256] = block.astype(BF)
+            wvt[pl.ds(a, 256), 256 * c:256 * c + 256] = jnp.transpose(wv[256 * c:256 * c + 256, pl.ds(a, 256)])
             yield
 
     def weave(*jobs):
@@ -176,31 +174,36 @@
 
     arrived(0)
     weave(normed(raw.at[0], y0))
-    w_copies[0].wait()
     w_copies[2].start()
+    w_copies[0].start()
 
     def norm_pair(i, carry):
         b = 2 * i
         arrived(b + 1)
         arrived(b + 2)
-        weave(permuted(y0, rows_of(b)), normed(raw.at[b + 1], y1), averaged(b), flip(pl.multiple_of(256 * i, 256)))
+        weave(permuted(y0, rows_of(b)), normed(raw.at[b + 1], y1), averaged(b))
         weave(permuted(y1, rows_of(b + 1)), normed(raw.at[b + 2], y0), averaged(b + 1))
         return carry
 
     lax.fori_loop(0, 3, norm_pair, 0)
     arrived(7)
-    weave(permuted(y0, rows_of(6)), normed(raw.at[7], y1), averaged(6), flip(768))
+    weave(permuted(y0, rows_of(6)), normed(raw.at[7], y1), averaged(6))
     weave(permuted(y1, rows_of(7)), averaged(7))
     w_copies[3].start()
 
+    w_copies[0].wait()
     w_copies[2].wait()
     scale = math.log2(math.e) / 8.0
 
-    def project_queries(i, carry):
+    def own_queries(i):
         rows = pl.ds(pl.multiple_of(512 * i, 512), 512)
         x = xn[pl.ds(4 * i, 4), 16:16 + COUNT, :].reshape(512, D)
         for c in range(2):
             queries[rows, 512 * c:512 * c + 512] = (nn(x, wq[:, 512 * c:512 * c + 512]) * scale).astype(BF)
+            yield
+
+    def project_queries(i, carry):
+        weave(own_queries(i), flip(pl.multiple_of(256 * i, 256)))
         return carry
 
     lax.fori_loop(0, 4, project_queries, 0)
@@ -309,16 +312,24 @@
         return carry
 
     lax.fori_loop(0, 3, attend, 0)
-    weave(probs_of(7, pr1), attended_of(6, pr0))
+    def project_out(jp):
+        att = []
+        for b in range(4):
+            pair = jnp.concatenate([acc[2 * jp, b], acc[2 * jp + 1, b]], axis=0)
+            turned = jnp.transpose(pair * (1.0 / PATCH)).astype(BF)
+            att.append(jnp.concatenate([turned[32 * h:32 * h + 32] for h in range(4)], axis=1))
+            yield
+        att = jnp.concatenate(att, axis=0)
+        for c in range(2):
+            tokmean[:, 512 * c:512 * c + 512] += nn(att, wo[512 * jp:512 * jp + 512, 512 * c:512 * c + 512])
+            yield
+
+    pltpu.make_async_copy(w_out, wo, w_sem.at[5]).wait()
+    weave(probs_of(7, pr1), attended_of(6, pr0), project_out(0))
     weave(attended_of(7, pr1))
-
-    pltpu.make_async_copy(w_out, wo, w_sem.at[5]).wait()
-    att = []
-    for b in range(4):
-        pairs = [jnp.concatenate([acc[2 * jp, b], acc[2 * jp + 1, b]], axis=0) for jp in range(2)]
-        turned = [jnp.transpose(pair * (1.0 / PATCH)).astype(BF) for pair in pairs]
-        att.append(jnp.concatenate([t[32 * h:32 * h + 32] for t in turned for h in range(4)], axis=1))
-    pooled = tokmean[...] + nn(jnp.concatenate(att, axis=0), wo[...])
+    weave(project_out(1))
+
+    pooled = tokmean[...]
     blocks = pooled.reshape(VIDS, PART, D)
     pack[...] = jnp.concatenate([blocks[:, :, :HALF], blocks[:, :, HALF:]], axis=1).astype(BF)
 

time: 53.3 us -> 52.8 us (level)
    pallas_call x1, Pallas kernels: 50.7 us -> 50.1 us  [local(): pl.pallas_call(kernel, out_shape=(jax.ShapeDtypeStruct((COUNT, E), BF), j...]
where the time goes in v7:
time: 52.8 us; the launch traced here: 52.6 us
  Pallas kernels  52 us (98%)
  between operations  0.64 us (1%)
    pallas_call x1, Pallas kernels, local(): pl.pallas_call(kernel, out_shape=(jax.ShapeDtypeStruct((COUNT, E), BF), j...  50.1 us
    pallas_call x1, Pallas kernels, local(): pl.pallas_call(hand_over, out_shape=(jax.ShapeDtypeStruct((COUNT, E), BF)...  1.87 us

profile of v7, /device:TPU:1, one launch (start us, length us, event | category | flops | bytes accessed | tf_op | source)
XLA Modules:
  0.0 52.6 jit_solution(12601814262212393309)
XLA Ops:
  0.6 50.1 %shard_map.95 = (bf16[128,2048]{1,0:T(8,128)(2,1)}, f32[1,128]{1,0:T(1,128)}) custom-call(s32[16]{0:T(128)} %valid.1, bf16[2048,1024]{1,0:T(8,128)(2,1)} %bitcast.4, f32[1,1024]{1,0:T(1,128)} %bitcast.6, bf16[1024,3072]{1,0:T(8,128)(2,1)} %w_qkv.1, bf16[1024,1024]{1,0:T(8,128)(2,1)} %w_out.1, bf16[1024,2048]{1,0:T(8,128)(2,1)} %w_proj.1, s32[1,128]{1,0:T(1,128)} %offsets.1, ...), custom_call_target="tpu_custom_call" | custom-call | tf_op jit(solution)/shard_map/pallas_call | solution.py:433
  50.7 1.9 %shard_map.96 = (bf16[128,2048]{1,0:T(8,128)(2,1)}, f32[1,128]{1,0:T(1,128)}) custom-call(bf16[128,2048]{1,0:T(8,128)(2,1)} %get-tuple-element.6.emb, f32[1,128]{1,0:T(1,128)} %get-tuple-element.7.losses), custom_call_target="tpu_custom_call" | custom-call | tf_op jit(solution)/shard_map/pallas_call | solution.py:493

commit v8 on v7

--- a/solution.py
+++ b/solution.py
@@ -71,24 +71,18 @@
             ]
         )
     ]
+    w_copies[1].start()
+    tok_copies[0].start()
+    for copy in tok_copies[1:]:
+        copy.start()
     out_copies = [
-        pltpu.make_async_copy(
-            w_out.at[pl.ds(256 * (2 * jp + j2) + 64 * h, 64)],
-            wo.at[pl.ds(512 * jp + 128 * h + 64 * j2, 64)],
-            w_sem.at[5],
-        )
-        for jp in range(2) for h in range(4) for j2 in range(2)
+        pltpu.make_async_copy(w_out.at[jp, j2], wo.at[jp, :, j2], w_sem.at[5]) for jp in range(2) for j2 in range(2)
     ]
     barrier = pltpu.get_barrier_semaphore()
     for peer in peers:
         pl.semaphore_signal(barrier, inc=1, device_id=peer, device_id_type=MESH)
     for peer in (left, right):
         pl.semaphore_signal(barrier, inc=1, device_id={"tm": peer}, device_id_type=MESH)
-    w_copies[1].start()
-    tok_copies[0].start()
-    for copy in tok_copies[1:]:
-        copy.start()
-
     r0, r1 = iota((256, 256), 0), iota((256, 256), 1)
     perm[...] = (r1 == (r0 % 16) * 16 + r0 // 16).astype(F32).astype(BF)
     eye[...] = (r0 == r1).astype(F32).astype(BF)
@@ -321,10 +315,10 @@
             yield
         att = jnp.concatenate(att, axis=0)
         for c in range(2):
-            tokmean[:, 512 * c:512 * c + 512] += nn(att, wo[512 * jp:512 * jp + 512, 512 * c:512 * c + 512])
-            yield
-
-    pltpu.make_async_copy(w_out, wo, w_sem.at[5]).wait()
+            tokmean[:, 512 * c:512 * c + 512] += nn(att, wo[jp, :, :, :, 512 * c:512 * c + 512].reshape(512, 512))
+            yield
+
+    pltpu.make_async_copy(wo, wo, w_sem.at[5]).wait()
     weave(probs_of(7, pr1), attended_of(6, pr0), project_out(0))
     weave(attended_of(7, pr1))
     weave(project_out(1))
@@ -364,15 +358,15 @@
     e = own_e[...]
     near_own = nt(e, e)
 
-    for copy in near_copies:
-        copy.wait_recv()
+    def embedded(blocks):
+        seen = blocks.astype(F32)
+        seen = jnp.concatenate([seen[:, :PART], seen[:, PART:]], axis=2)
+        return nn(seen.reshape(-1, D).astype(BF), wp[...]).astype(BF)
+
     pltpu.make_async_copy(got, got, a_recv).wait()
-    seen = jnp.concatenate([got[...], near[...]], axis=0).astype(F32)
-    seen = jnp.concatenate([seen[:, :PART], seen[:, PART:]], axis=2)
-    seen = seen.reshape((VIDS + 2) * PART, D).astype(BF)
-    all_e = nn(seen, wp[...]).astype(BF)
+    all_e = embedded(got[...])
     factor = 8.0 / math.sqrt(E)
-    gram = nt(all_e[:COUNT], all_e[:COUNT]) * factor
+    gram = nt(all_e, all_e) * factor
 
     frame_here = across * COUNT + PART * vid + lane % PART
     other = jnp.zeros((COUNT, COUNT), I32)
@@ -397,7 +391,9 @@
     for copy in back_copies:
         copy.start()
 
-    near_e = nt(all_e[COUNT:], e)
+    for copy in near_copies:
+        copy.wait_recv()
+    near_e = nt(embedded(near[...]), e)
     scores = jnp.concatenate([near_e[:REACH], near_own, near_e[REACH:]], axis=0)
     off = offsets[...]
     here = first + iota((1, COUNT), 1)
@@ -449,7 +445,7 @@
             pltpu.VMEM((D, D), BF),
             pltpu.VMEM((D, D), BF),
             pltpu.VMEM((D, D), BF),
-            pltpu.VMEM((D, D), BF),
+            pltpu.VMEM((2, 4, 2, 64, D), BF),
             pltpu.VMEM((D, E), BF),
             pltpu.VMEM((VIDS, NEG, COUNT), I32),
             pltpu.VMEM((COUNT, VIDS * NEG), F32),
@@ -485,7 +481,7 @@
         tokens.reshape(COUNT * PATCH, D),
         norm_gain.reshape(1, D),
         w_qkv,
-        w_out,
+        w_out.reshape(2, 2, 4, 64, D),
         w_proj,
         offsets,
         jnp.swapaxes(negatives, 1, 2),

time: 52.8 us -> 52.8 us (level)
  no operation moved by 1% of the time
where the time goes in v8:
time: 52.8 us; the launch traced here: 52.6 us
  Pallas kernels  52 us (98%)
  between operations  0.64 us (1%)
    pallas_call x1, Pallas kernels, local(): pl.pallas_call(kernel, out_shape=(jax.ShapeDtypeStruct((COUNT, E), BF), j...  50.1 us
    pallas_call x1, Pallas kernels, local(): pl.pallas_call(hand_over, out_shape=(jax.ShapeDtypeStruct((COUNT, E), BF)...  1.87 us

profile of v8, /device:TPU:1, one launch (start us, length us, event | category | flops | bytes accessed | tf_op | source)
XLA Modules:
  0.0 52.6 jit_solution(4445615408362482160)
XLA Ops:
  0.6 50.1 %shard_map.95 = (bf16[128,2048]{1,0:T(8,128)(2,1)}, f32[1,128]{1,0:T(1,128)}) custom-call(s32[16]{0:T(128)} %valid.1, bf16[2048,1024]{1,0:T(8,128)(2,1)} %bitcast.5, f32[1,1024]{1,0:T(1,128)} %bitcast.8, bf16[1024,3072]{1,0:T(8,128)(2,1)} %w_qkv.1, bf16[2,2,4,64,1024]{4,3,2,1,0:T(8,128)(2,1)} %bitcast.6, bf16[1024,2048]{1,0:T(8,128)(2,1)} %w_proj.1, ...), custom_call_target="tpu_custom_call" | custom-call | tf_op jit(solution)/shard_map/pallas_call | solution.py:429
  50.7 1.9 %shard_map.96 = (bf16[128,2048]{1,0:T(8,128)(2,1)}, f32[1,128]{1,0:T(1,128)}) custom-call(bf16[128,2048]{1,0:T(8,128)(2,1)} %get-tuple-element.6.emb, f32[1,128]{1,0:T(1,128)} %get-tuple-element.7.losses), custom_call_target="tpu_custom_call" | custom-call | tf_op jit(solution)/shard_map/pallas_call | solution.py:489

commit v9 on v8

--- a/solution.py
+++ b/solution.py
@@ -98,7 +98,114 @@
         bias[b] = jnp.where(ok, 0.0, -1e30)
     lane_block = iota((64, 128), 1) // 32
 
+    pl.semaphore_wait(barrier, VIDS + 2)
+
+    halo_copies = [
+        pltpu.make_async_remote_copy(
+            src_ref=tokens.at[pl.ds(256 * 7, 256)], dst_ref=halo.at[0],
+            send_sem=halo_send.at[0], recv_sem=halo_recv.at[0],
+            device_id={"tm": right}, device_id_type=MESH,
+        ),
+        pltpu.make_async_remote_copy(
+            src_ref=tokens.at[pl.ds(0, 256)], dst_ref=halo.at[1],
+            send_sem=halo_send.at[1], recv_sem=halo_recv.at[1],
+            device_id={"tm": left}, device_id_type=MESH,
+        ),
+    ]
+    for copy in halo_copies:
+        copy.start()
+
+    def normed(block, out, rows=(0, 1, 2, 3)):
+        for c in rows:
+            for n in range(4):
+                at = 64 * c + 16 * n
+                x = block[at:at + 16, :].astype(F32)
+                mean = jnp.sum(x * x, axis=1, keepdims=True) * (1.0 / D)
+                out[at:at + 16, :] = (x * lax.rsqrt(mean + 1e-5) * gain[...]).astype(BF)
+            yield
+
+    def permuted(y, rows):
+        for c in range(4):
+            part = nn(perm[...], y[:, 256 * c:256 * c + 256]).astype(BF)
+            xn[:, rows, 256 * c:256 * c + 256] = part.reshape(PATCH, 16, 256)
+            yield
+
+    def averaged(b):
+        tokmean[pl.ds(pl.multiple_of(16 * b, 16), 16), :] = nn(avg[...], raw[b])
+        yield
+
+    def rows_of(b):
+        return pl.ds(pl.multiple_of(16 * b + 16, 16), 16)
+
+    def flip(a):
+        for c in range(4):
+            wvt[pl.ds(a, 256), 256 * c:256 * c + 256] = jnp.transpose(wv[256 * c:256 * c + 256, pl.ds(a, 256)])
+            yield
+
+    def weave(*jobs):
+        for _ in itertools.zip_longest(*jobs):
+            pass
+
+    def arrived(b):
+        pltpu.make_async_copy(tokens.at[pl.ds(0, 256)], raw.at[b], tok_sem.at[b]).wait()
+
+    arrived(0)
+    weave(normed(raw.at[0], y0))
+    w_copies[2].start()
+    w_copies[0].start()
+
+    def norm_pair(i, carry):
+        b = 2 * i
+        arrived(b + 1)
+        arrived(b + 2)
+        weave(permuted(y0, rows_of(b)), normed(raw.at[b + 1], y1), averaged(b))
+        weave(permuted(y1, rows_of(b + 1)), normed(raw.at[b + 2], y0), averaged(b + 1))
+        return carry
+
+    lax.fori_loop(0, 3, norm_pair, 0)
+    arrived(7)
+    weave(permuted(y0, rows_of(6)), normed(raw.at[7], y1), averaged(6))
+    weave(permuted(y1, rows_of(7)), averaged(7))
+    w_copies[3].start()
+
+    w_copies[0].wait()
+    w_copies[2].wait()
+    scale = math.log2(math.e) / 8.0
+
+    def own_queries(i):
+        rows = pl.ds(pl.multiple_of(512 * i, 512), 512)
+        x = xn[pl.ds(4 * i, 4), 16:16 + COUNT, :].reshape(512, D)
+        for c in range(2):
+            queries[rows, 512 * c:512 * c + 512] = (nn(x, wq[:, 512 * c:512 * c + 512]) * scale).astype(BF)
+            yield
+
+    def project_queries(i, carry):
+        weave(own_queries(i), flip(pl.multiple_of(256 * i, 256)))
+        return carry
+
+    lax.fori_loop(0, 4, project_queries, 0)
+
+    for copy in w_copies[4:] + out_copies:
+        copy.start()
+
+    def values(ga, ra, gb, rb):
+        xa = xn[pl.ds(4 * ga, 4), 32 * ra:32 * ra + 32, :].reshape(128, D)
+        xb = xn[pl.ds(4 * gb, 4), 32 * rb:32 * rb + 32, :].reshape(128, D)
+        x2 = jnp.concatenate([xa, xb], axis=0)
+        for c in range(2):
+            r = nt(wvt[512 * c:512 * c + 512], x2).astype(BF)
+            vt[ga, 512 * c:512 * c + 512, 128 * ra:128 * ra + 128] = r[:, :128]
+            vt[gb, 512 * c:512 * c + 512, 128 * rb:128 * rb + 128] = r[:, 128:]
+            yield
+
+    def values_inner(i, carry):
+        weave(values(2 * i, 1, 2 * i, 2))
+        weave(values(2 * i + 1, 1, 2 * i + 1, 2))
+        return carry
+
     w_copies[1].wait()
+    lax.fori_loop(0, 2, values_inner, 0)
+
     lane = iota((COUNT, COUNT), 1)
     row = iota((COUNT, COUNT), 0)
     negt[...] = jnp.transpose(negs[...].reshape(VIDS * NEG, COUNT).astype(F32))
@@ -109,121 +216,12 @@
         one = jnp.sum(jnp.where(lane == row // PART * NEG + k, ids, 0.0), axis=1, keepdims=True)
         times += (one * PART + (row % PART).astype(F32) == lane.astype(F32)).astype(F32)
     count_out[...] = times
-
-    pl.semaphore_wait(barrier, VIDS + 2)
-
-    halo_copies = [
-        pltpu.make_async_remote_copy(
-            src_ref=tokens.at[pl.ds(256 * 7, 256)], dst_ref=halo.at[0],
-            send_sem=halo_send.at[0], recv_sem=halo_recv.at[0],
-            device_id={"tm": right}, device_id_type=MESH,
-        ),
-        pltpu.make_async_remote_copy(
-            src_ref=tokens.at[pl.ds(0, 256)], dst_ref=halo.at[1],
-            send_sem=halo_send.at[1], recv_sem=halo_recv.at[1],
-            device_id={"tm": left}, device_id_type=MESH,
-        ),
-    ]
-    for copy in halo_copies:
-        copy.start()
-
+    weave(values(0, 3, 1, 3))
+    weave(values(2, 3, 3, 3))
     count_copy = pltpu.make_async_remote_copy(
         src_ref=count_out, dst_ref=count, send_sem=c_send, recv_sem=c_recv, device_id=peers[-1], device_id_type=MESH,
     )
     count_copy.start()
-
-    def normed(block, out, rows=(0, 1, 2, 3)):
-        for c in rows:
-            for n in range(4):
-                at = 64 * c + 16 * n
-                x = block[at:at + 16, :].astype(F32)
-                mean = jnp.sum(x * x, axis=1, keepdims=True) * (1.0 / D)
-                out[at:at + 16, :] = (x * lax.rsqrt(mean + 1e-5) * gain[...]).astype(BF)
-            yield
-
-    def permuted(y, rows):
-        for c in range(4):
-            part = nn(perm[...], y[:, 256 * c:256 * c + 256]).astype(BF)
-            xn[:, rows, 256 * c:256 * c + 256] = part.reshape(PATCH, 16, 256)
-            yield
-
-    def averaged(b):
-        tokmean[pl.ds(pl.multiple_of(16 * b, 16), 16), :] = nn(avg[...], raw[b])
-        yield
-
-    def rows_of(b):
-        return pl.ds(pl.multiple_of(16 * b + 16, 16), 16)
-
-    def flip(a):
-        for c in range(4):
-            wvt[pl.ds(a, 256), 256 * c:256 * c + 256] = jnp.transpose(wv[256 * c:256 * c + 256, pl.ds(a, 256)])
-            yield
-
-    def weave(*jobs):
-        for _ in itertools.zip_longest(*jobs):
-            pass
-
-    def arrived(b):
-        pltpu.make_async_copy(tokens.at[pl.ds(0, 256)], raw.at[b], tok_sem.at[b]).wait()
-
-    arrived(0)
-    weave(normed(raw.at[0], y0))
-    w_copies[2].start()
-    w_copies[0].start()
-
-    def norm_pair(i, carry):
-        b = 2 * i
-        arrived(b + 1)
-        arrived(b + 2)
-        weave(permuted(y0, rows_of(b)), normed(raw.at[b + 1], y1), averaged(b))
-        weave(permuted(y1, rows_of(b + 1)), normed(raw.at[b + 2], y0), averaged(b + 1))
-        return carry
-
-    lax.fori_loop(0, 3, norm_pair, 0)
-    arrived(7)
-    weave(permuted(y0, rows_of(6)), normed(raw.at[7], y1), averaged(6))
-    weave(permuted(y1, rows_of(7)), averaged(7))
-    w_copies[3].start()
-
-    w_copies[0].wait()
-    w_copies[2].wait()
-    scale = math.log2(math.e) / 8.0
-
-    def own_queries(i):
-        rows = pl.ds(pl.multiple_of(512 * i, 512), 512)
-        x = xn[pl.ds(4 * i, 4), 16:16 + COUNT, :].reshape(512, D)
-        for c in range(2):
-            queries[rows, 512 * c:512 * c + 512] = (nn(x, wq[:, 512 * c:512 * c + 512]) * scale).astype(BF)
-            yield
-
-    def project_queries(i, carry):
-        weave(own_queries(i), flip(pl.multiple_of(256 * i, 256)))
-        return carry
-
-    lax.fori_loop(0, 4, project_queries, 0)
-
-    for copy in w_copies[4:] + out_copies:
-        copy.start()
-
-    def values(ga, ra, gb, rb):
-        xa = xn[pl.ds(4 * ga, 4), 32 * ra:32 * ra + 32, :].reshape(128, D)
-        xb = xn[pl.ds(4 * gb, 4), 32 * rb:32 * rb + 32, :].reshape(128, D)
-        x2 = jnp.concatenate([xa, xb], axis=0)
-        for c in range(2):
-            r = nt(wvt[512 * c:512 * c + 512], x2).astype(BF)
-            vt[ga, 512 * c:512 * c + 512, 128 * ra:128 * ra + 128] = r[:, :128]
-            vt[gb, 512 * c:512 * c + 512, 128 * rb:128 * rb + 128] = r[:, 128:]
-            yield
-
-    def values_inner(i, carry):
-        weave(values(2 * i, 1, 2 * i, 2))
-        weave(values(2 * i + 1, 1, 2 * i + 1, 2))
-        return carry
-
-    lax.fori_loop(0, 2, values_inner, 0)
-
-    weave(values(0, 3, 1, 3))
-    weave(values(2, 3, 3, 3))
 
     w_copies[3].wait()
 

time: 52.8 us -> 52.9 us (level)
  no operation moved by 1% of the time
where the time goes in v9:
time: 52.9 us; the launch traced here: 52.7 us
  Pallas kernels  52.1 us (98%)
  between operations  0.64 us (1%)
    pallas_call x1, Pallas kernels, local(): pl.pallas_call(kernel, out_shape=(jax.ShapeDtypeStruct((COUNT, E), BF), j...  50.2 us
    pallas_call x1, Pallas kernels, local(): pl.pallas_call(hand_over, out_shape=(jax.ShapeDtypeStruct((COUNT, E), BF)...  1.87 us

profile of v9, /device:TPU:1, one launch (start us, length us, event | category | flops | bytes accessed | tf_op | source)
XLA Modules:
  0.0 52.7 jit_solution(15912496827384526974)
XLA Ops:
  0.6 50.2 %shard_map.95 = (bf16[128,2048]{1,0:T(8,128)(2,1)}, f32[1,128]{1,0:T(1,128)}) custom-call(s32[16]{0:T(128)} %valid.1, bf16[2048,1024]{1,0:T(8,128)(2,1)} %bitcast.5, f32[1,1024]{1,0:T(1,128)} %bitcast.8, bf16[1024,3072]{1,0:T(8,128)(2,1)} %w_qkv.1, bf16[2,2,4,64,1024]{4,3,2,1,0:T(8,128)(2,1)} %bitcast.6, bf16[1024,2048]{1,0:T(8,128)(2,1)} %w_proj.1, ...), custom_call_target="tpu_custom_call" | custom-call | tf_op jit(solution)/shard_map/pallas_call | solution.py:427
  50.8 1.9 %shard_map.96 = (bf16[128,2048]{1,0:T(8,128)(2,1)}, f32[1,128]{1,0:T(1,128)}) custom-call(bf16[128,2048]{1,0:T(8,128)(2,1)} %get-tuple-element.6.emb, f32[1,128]{1,0:T(1,128)} %get-tuple-element.7.losses), custom_call_target="tpu_custom_call" | custom-call | tf_op jit(solution)/shard_map/pallas_call | solution.py:487
